TPU v7x, 256 devices: a whole 4x4x8 slice. The times are simulated.
256 devices in a mesh: group: 4 (over x_lo, core), dp: 8 (over z), tensor: 8 (over x_hi, y).
Axes of the slice: x: 4 (x_hi: 2, x_lo: 2; x = x_hi * 2 + x_lo), y: 4, z: 8, core: 2. Of those that a mesh axis runs over, the one named last changes fastest.
Arguments:
- images: float32 [8, 1024, 588], P('dp', 'tensor'), may hold values from 0 to 1
- step_size: float32 [8], P('dp'), may hold values from 0.05 to 0.25
- member_mask: int32 [4, 8], P('group', 'dp'), may hold values 0 or 1
- patch_weight: bfloat16 [4, 588, 1280], P('group'), may hold values from -0.25 to 0.25
- vision_norm_gain: float32 [4, 1280], P('group'), may hold values from 0.5 to 1.5
- merger_weight: bfloat16 [4, 5120, 8192], P('group', 'dp', 'tensor')
- norm_gain: float32 [4, 8192], P('group'), may hold values from 0.5 to 1.5
- kv_weight: bfloat16 [4, 2, 8192, 1024], P('group', None, 'dp', 'tensor'), may hold values from -0.0625 to 0.0625
- queries: bfloat16 [4, 8, 32, 8192], P('group', 'dp', None, 'tensor'), may hold values from -6 to 6
- cotangent: bfloat16 [4, 8, 32, 8192], P('group', 'dp', None, 'tensor'), may hold values from -6 to 6
Outputs:
- adversarial: float32 [8, 1024, 588], P('dp', 'tensor')
- direction: float32 [8, 1024, 588], P('dp', 'tensor')
All inputs are finite; a program needn't handle non-finite values. No bound on the sum of `member_mask` on one device may be relied on, other than what follows from the above.
Results may differ from a plain program's by a relative error of at most 0.025.
Values may be sent and summed in bfloat16 or wider, within the bound.
A program may use at most 128 MiB of HBM per device.

v0:
```python
import math

import jax
import jax.numpy as jnp
from jax import lax
from jax.sharding import PartitionSpec as P

P_SIZE = 588
D = 8192
H = 64
KVH = 8
HD = 128
NP = 1024


def body(
    images,
    step_size,
    member_mask,
    patch_weight,
    vision_norm_gain,
    merger_weight,
    norm_gain,
    kv_weight,
    queries,
    cotangent,
):
    count = images.shape[0]
    scale = 1.0 / math.sqrt(HD)
    pixels = images.astype(jnp.bfloat16)
    patch_w = patch_weight[0]
    embed = jnp.einsum("inp,pv->inv", pixels, patch_w, preferred_element_type=jnp.float32)
    centered_rows = embed - jnp.mean(embed, -1, keepdims=True)
    inverse_deviation = lax.rsqrt(
        jnp.mean(centered_rows * centered_rows, -1, keepdims=True) + 1e-06
    )
    normalized_input = centered_rows * inverse_deviation
    visual_features = (normalized_input * vision_norm_gain[0]).astype(jnp.bfloat16)
    merged = visual_features.reshape(count, images.shape[1] // 4, 4 * visual_features.shape[2])
    merged_all = lax.all_gather(merged, "tensor", axis=1, tiled=True)
    merger_w = merger_weight[0]
    merger_full = lax.all_gather(merger_w, "dp", axis=0, tiled=True)
    hidden_sum = jnp.einsum(
        "itr,rc->itc", merged_all, merger_full, preferred_element_type=jnp.float32
    )
    hidden_bf = hidden_sum.astype(jnp.bfloat16)
    hidden_own = hidden_bf.astype(jnp.float32)
    gain = norm_gain[0]
    width = hidden_bf.shape[2]
    gain_own = lax.dynamic_slice_in_dim(gain, lax.axis_index("tensor") * width, width, 0)
    total_sq = lax.psum(jnp.sum(hidden_own * hidden_own, -1, keepdims=True), "tensor")
    root = lax.rsqrt(total_sq / D + 1e-06)
    features_own = (hidden_own * root * gain_own).astype(jnp.bfloat16)
    kv_gathered = lax.all_gather(kv_weight[0], "dp", axis=1, tiled=True)
    features = lax.all_gather(features_own, "tensor", axis=2, tiled=True)
    keys_bf = jnp.einsum(
        "itr,rc->itc", features, kv_gathered[0], preferred_element_type=jnp.float32
    ).astype(jnp.bfloat16)
    values_bf = jnp.einsum(
        "itr,rc->itc", features, kv_gathered[1], preferred_element_type=jnp.float32
    ).astype(jnp.bfloat16)
    heads_kv = keys_bf.shape[2] // HD
    group_heads = H // KVH
    tokens = keys_bf.shape[1]
    query = queries[0].reshape(count, queries.shape[2], heads_kv, group_heads, HD)
    key_heads = keys_bf.reshape(count, tokens, heads_kv, HD)
    value_heads = values_bf.reshape(count, tokens, heads_kv, HD)
    scores = (
        jnp.einsum("icagd,itad->iagct", query, key_heads, preferred_element_type=jnp.float32)
        * scale
    )
    probs = jax.nn.softmax(scores, axis=-1)
    probs_bf = probs.astype(jnp.bfloat16)
    weight_mask = member_mask[0].astype(jnp.bfloat16)[:, None, None]
    grad_out = (cotangent[0] * weight_mask).reshape(query.shape)
    grad_probs = jnp.einsum(
        "icagd,itad->iagct", grad_out, value_heads, preferred_element_type=jnp.float32
    )
    inner = jnp.sum(probs * grad_probs, -1, keepdims=True)
    grad_scores = (probs * (grad_probs - inner) * scale).astype(jnp.bfloat16)
    grad_values = (
        jnp.einsum("iagct,icagd->itad", probs_bf, grad_out, preferred_element_type=jnp.float32)
        .astype(jnp.bfloat16)
        .reshape(keys_bf.shape)
    )
    grad_keys = (
        jnp.einsum("iagct,icagd->itad", grad_scores, query, preferred_element_type=jnp.float32)
        .astype(jnp.bfloat16)
        .reshape(keys_bf.shape)
    )
    partial_value = jnp.einsum(
        "itc,rc->itr", grad_keys, kv_gathered[0], preferred_element_type=jnp.float32
    )
    partial_value = partial_value + jnp.einsum(
        "itc,rc->itr", grad_values, kv_gathered[1], preferred_element_type=jnp.float32
    )
    grad_feat = lax.psum_scatter(partial_value, "tensor", scatter_dimension=2, tiled=True)
    row_sum = lax.psum(jnp.sum(grad_feat * gain_own * hidden_own, -1, keepdims=True), "tensor")
    grad_hidden = (root * gain_own * grad_feat - hidden_own * root**3 * row_sum / D).astype(
        jnp.bfloat16
    )
    merged_terms = jnp.einsum(
        "itc,rc->itr", grad_hidden, merger_full, preferred_element_type=jnp.float32
    )
    grad_merged = lax.psum_scatter(merged_terms, "tensor", scatter_dimension=1, tiled=True)
    grad_visual = grad_merged.reshape(embed.shape)
    gain_gradient = grad_visual * vision_norm_gain[0]
    embedding_gradient = (
        inverse_deviation
        * (
            gain_gradient
            - jnp.mean(gain_gradient, -1, keepdims=True)
            - normalized_input * jnp.mean(gain_gradient * normalized_input, -1, keepdims=True)
        )
    ).astype(jnp.bfloat16)
    grad_pixels = jnp.einsum(
        "inv,pv->inp", embedding_gradient, patch_w, preferred_element_type=jnp.float32
    )
    gradient = lax.psum(grad_pixels, "group")
    squares = lax.psum(jnp.sum(gradient * gradient, axis=(1, 2)), "tensor")
    direction = jnp.tanh(gradient * lax.rsqrt(squares / (NP * P_SIZE) + 1e-06)[:, None, None])
    adversarial = jnp.clip(images + step_size[:, None, None] * direction, 0.0, 1.0)
    return (adversarial, direction)


def solution(mesh):
    placed = (
        P("dp", "tensor", None),
        P("dp"),
        P("group", "dp"),
        P("group", None, None),
        P("group", None),
        P("group", "dp", "tensor"),
        P("group", None),
        P("group", None, "dp", "tensor"),
        P("group", "dp", None, "tensor"),
        P("group", "dp", None, "tensor"),
    )
    return jax.shard_map(
        body,
        mesh=mesh,
        in_specs=placed,
        out_specs=(P("dp", "tensor", None), P("dp", "tensor", None)),
        check_vma=False,
    )
```

profile of v0, /device:TPU:1, one launch (start us, length us, event | category | flops | bytes accessed | tf_op | source)
XLA Modules:
  0.0 672.3 jit_solution(15675611040948301334)
XLA Ops:
  7.2 0.0 copy-start
  7.2 0.0 all-gather.8.cloned.1.call-start
  7.2 1.3 convert_element_type.69
  8.5 0.1 copy-done
  8.6 0.5 fusion.77
  9.2 0.2 multiply_reduce_fusion.2
  9.4 0.7 reduce.14
  10.1 0.2 multiply_convert_fusion.1
  10.3 1.0 reshape.293
  11.3 0.0 all-gather.8.cloned.1.call-update
  11.3 0.0 all-gather.10.cloned.1.call-start
  11.3 0.7 all-gather.10.cloned.1.call-update
  12.1 0.0 all-gather.14.cloned.1.call-start
  12.1 0.7 all-gather.14.cloned.1.call-update
  12.8 0.0 all-gather.12.cloned.1.call-start
  12.8 0.7 constant_dynamic-slice_fusion
  13.5 0.0 copy-start.2
  13.5 0.0 copy-start.3
  13.5 64.8 %all-gather.8.cloned.1.call-done = bf16[1,256,5120]{2,1,0:T(8,128)(2,1)} async-done(((bf16[1,32,5120]{2,1,0:T(8,128)(2,1)}), bf16[1,256,5120]{2,1,0:T(8,128)(2,1)}) %all-gather.8.cloned.1.call-update) | async-done | bytes 2621456 | tf_op jit(solution)/shard_map/all_gather | solution.py:40
  78.3 114.0 %all-gather.10.cloned.1.call-done = bf16[1,5120,1024]{2,1,0:T(8,128)(2,1)} async-done(((bf16[1,640,1024]{2,1,0:T(8,128)(2,1)}), bf16[1,5120,1024]{2,1,0:T(8,128)(2,1)}) %all-gather.10.cloned.1.call-update) | async-done | bytes 10485776 | tf_op jit(solution)/shard_map/all_gather | solution.py:42
  192.3 7.7 %fusion.32 = (f32[256]{0:T(256)S(1)}, bf16[256,1024]{1,0:T(8,128)(2,1)S(1)}) fusion(bf16[1,5120,1024]{2,1,0:T(8,128)(2,1)} %all-gather.10.cloned.1.call-done, bf16[1,256,5120]{2,1,0:T(8,128)(2,1)} %all-gather.8.cloned.1.call-done), kind=kOutput, calls=%fused_computation.35 | convolution fusion | flops 2685402880 | bytes 13632512 | tf_op jit(solution)/shard_map/itr,rc->itc/dot_general | solution.py:43
  200.0 20.4 %psum.28 = f32[1,256,1]{1,2,0:T(1,128)S(1)} all-reduce(f32[1,256,1]{1,2,0:T(1,128)S(1)} %bitcast.163), channel_id=1, replica_groups=mesh['group'=4,'dp'=8,'tensor'=8] {'tensor'}, use_global_device_ids=true, to_apply=%region_3.0 | all-reduce | flops 256 | bytes 2048 | tf_op jit(solution)/shard_map/psum | solution.py:51
  220.4 1.0 fusion.34
  221.4 0.0 all-gather.12.cloned.1.call-update
  221.4 0.0 reduce-scatter.3.cloned.1.call-start
  221.4 0.0 copy-done.2
  222.1 0.0 copy-done.3
  222.2 25.4 %all-gather.14.cloned.1.call-done = bf16[1,2,8192,128]{3,2,1,0:T(8,128)(2,1)} async-done(((bf16[1,2,1024,128]{3,2,1,0:T(8,128)(2,1)}), bf16[1,2,8192,128]{3,2,1,0:T(8,128)(2,1)}) %all-gather.14.cloned.1.call-update) | async-done | bytes 4194320 | tf_op jit(solution)/shard_map/all_gather | solution.py:54
  247.5 77.1 %all-gather.12.cloned.1.call-done = bf16[256,8192]{1,0:T(8,128)(2,1)} async-done(((bf16[256,1024]{1,0:T(8,128)(2,1)}), bf16[256,8192]{1,0:T(8,128)(2,1)}) %all-gather.12.cloned.1.call-update) | async-done | bytes 4194320 | tf_op jit(solution)/shard_map/all_gather | solution.py:55
  324.6 4.4 fusion.78
  329.1 0.2 fusion.56
  329.3 4.3 convolution_bitcast_fusion
  333.6 0.2 convert_bitcast_fusion.1
  333.8 6.5 fusion.9
  340.3 8.9 %fusion = f32[1,256,8192]{2,1,0:T(8,128)} fusion(f32[256,8192]{1,0:T(8,128)} %fusion.9, bf16[1,2,8192,128]{3,2,1,0:T(8,128)(2,1)} %all-gather.14.cloned.1.call-done, bf16[32,8,128]{2,1,0:T(8,128)(2,1)S(1)} %bitcast.153, bf16[8,32,256]{2,1,0:T(8,128)(2,1)S(1)} %get-tuple-element.10), kind=kOutput, calls=%fused_computation.1 | convolution fusion | flops 555778048 | bytes 19070976 | tf_op jit(solution)/shard_map/itc,rc->itr/dot_general | solution.py:94
  349.2 0.0 reduce-scatter.3.cloned.1.call-update
  349.2 0.0 reduce-scatter.5.cloned.1.call-start
  349.2 117.4 %reduce-scatter.3.cloned.1.call-done = f32[1,256,1024]{2,1,0:T(8,128)} async-done(((f32[1,256,8192]{2,1,0:T(8,128)}), f32[1,256,1024]{2,1,0:T(8,128)}) %reduce-scatter.3.cloned.1.call-update) | async-done | bytes 1048592 | tf_op jit(solution)/shard_map/reduce_scatter | solution.py:97
  466.6 1.5 fusion.41
  468.1 16.2 %psum.29 = f32[256]{0:T(256)S(1)} all-reduce(f32[256]{0:T(256)S(1)} %fusion.41), channel_id=1, replica_groups=mesh['group'=4,'dp'=8,'tensor'=8] {'tensor'}, use_global_device_ids=true, to_apply=%region_9.0 | all-reduce | flops 256 | bytes 2048 | tf_op jit(solution)/shard_map/psum | solution.py:98
  484.3 9.8 %fusion.5 = f32[1,256,5120]{2,1,0:T(8,128)} fusion(bf16[1,5120,1024]{2,1,0:T(8,128)(2,1)} %all-gather.10.cloned.1.call-done, bf16[256,1024]{1,0:T(8,128)(2,1)S(1)} %get-tuple-element.15, f32[1,256,1024]{2,1,0:T(8,128)} %reduce-scatter.3.cloned.1.call-done, f32[256]{0:T(256)S(1)} %psum.29, f32[256]{0:T(256)S(1)} %bitcast.162, f32[1024]{0:T(1024)S(1)} %bitcast.159, ...), kind=kOutput, calls=%fused_computation.6 | convolution fusion | flops 2686451712 | bytes 17308672 | tf_op jit(solution)/shard_map/itc,rc->itr/dot_general | solution.py:102
  494.1 0.0 reduce-scatter.5.cloned.1.call-update
  494.1 0.0 copy-start.1
  494.1 0.0 all-reduce.2.cloned.1.call-start
  494.1 98.9 %reduce-scatter.5.cloned.1.call-done = f32[1,32,5120]{2,1,0:T(8,128)} async-done(((f32[1,256,5120]{2,1,0:T(8,128)}), f32[1,32,5120]{2,1,0:T(8,128)}) %reduce-scatter.5.cloned.1.call-update) | async-done | bytes 655376 | tf_op jit(solution)/shard_map/reduce_scatter | solution.py:105
  593.0 1.3 reshape.303
  594.3 0.1 multiply_reduce_fusion.1
  594.4 1.3 reshape.302
  595.7 0.2 multiply_reduce_fusion
  596.0 1.4 fusion.21
  597.4 0.0 all-reduce.2.cloned.1.call-update
  598.1 41.2 %all-reduce.2.cloned.1.call-done = f32[1,128,588]{1,2,0:T(8,128)} async-done(((f32[1,128,588]{1,2,0:T(8,128)}), f32[1,128,588]{1,2,0:T(8,128)}) %all-reduce.2.cloned.1.call-update) | async-done | bytes 301072 | tf_op jit(solution)/shard_map/psum | solution.py:119
  639.3 1.6 multiply_reduce_fusion.3
  641.0 20.7 %psum.31 = f32[1]{0:T(128)} all-reduce(f32[1]{0:T(128)} %bitcast.36), channel_id=1, replica_groups=mesh['group'=4,'dp'=8,'tensor'=8] {'tensor'}, use_global_device_ids=true, to_apply=%region_15.0 | all-reduce | flops 1 | bytes 8 | tf_op jit(solution)/shard_map/psum | solution.py:120
  662.3 0.0 copy-done.1
  662.4 1.0 fusion.54
  663.4 1.0 copy.24
  664.4 1.0 copy.25
  (7 shorter events, 0.1 us)
Async XLA Ops:
  7.2 1.5 copy-start
  7.2 71.1 %all-gather.8.cloned.1.call-start = ((), (), s32[]{:S(2)}) async-start(), calls=%async_computation.2 | async-start | bytes 2949120 | tf_op jit(solution)/shard_map/all_gather | solution.py:40
  11.3 181.0 %all-gather.10.cloned.1.call-start = ((), (), s32[]{:S(2)}) async-start(), calls=%async_computation.6 | async-start | bytes 11796480 | tf_op jit(solution)/shard_map/all_gather | solution.py:42
  12.1 235.5 %all-gather.14.cloned.1.call-start = ((), (), s32[]{:S(2)}) async-start(), calls=%async_computation.8 | async-start | bytes 4718592 | tf_op jit(solution)/shard_map/all_gather | solution.py:54
  12.8 311.9 %all-gather.12.cloned.1.call-start = ((), (), s32[]{:S(2)}) async-start(), calls=%async_computation.7 | async-start | bytes 4718592 | tf_op jit(solution)/shard_map/all_gather | solution.py:55
  13.5 207.9 %copy-start.2 = (bf16[1,1,32,1024]{3,2,1,0:T(8,128)(2,1)S(1)}, bf16[1,1,32,1024]{3,2,1,0:T(8,128)(2,1)}, u32[]{:S(2)}) copy-start(bf16[1,1,32,1024]{3,2,1,0:T(8,128)(2,1)} %param.18) | copy-start | bytes 196612
  13.5 208.6 %copy-start.3 = (bf16[1,1,32,1024]{3,2,1,0:T(8,128)(2,1)S(1)}, bf16[1,1,32,1024]{3,2,1,0:T(8,128)(2,1)}, u32[]{:S(2)}) copy-start(bf16[1,1,32,1024]{3,2,1,0:T(8,128)(2,1)} %param.19) | copy-start | bytes 196612
  221.4 245.2 %reduce-scatter.3.cloned.1.call-start = ((), (), s32[]{:S(2)}) async-start(), calls=%async_computation.3 | async-start | bytes 9437184 | tf_op jit(solution)/shard_map/reduce_scatter | solution.py:97
  349.2 243.8 %reduce-scatter.5.cloned.1.call-start = ((), (), s32[]{:S(2)}) async-start(), calls=%async_computation.4 | async-start | bytes 5898240 | tf_op jit(solution)/shard_map/reduce_scatter | solution.py:105
  494.1 168.3 %copy-start.1 = (f32[1,128,588]{1,0,2:T(1,128)S(1)}, f32[1,128,588]{1,0,2:T(1,128)}, u32[]{:S(2)}) copy-start(f32[1,128,588]{1,0,2:T(1,128)} %param.10) | copy-start | bytes 903172
  494.1 145.2 %all-reduce.2.cloned.1.call-start = ((), (), s32[]{:S(2)}) async-start(), calls=%async_computation.5 | async-start | bytes 606208 | tf_op jit(solution)/shard_map/psum | solution.py:119
Sparse Core Ops, SparseCore 0:
  11.4 66.8 all-gather.7
  80.1 112.1 all-gather.9
  194.1 53.4 all-gather.13
  250.0 74.6 all-gather.11
  349.3 117.2 reduce-scatter.2
  494.2 98.7 reduce-scatter.4
  597.6 41.7 all-reduce.1
where the time goes:
time: 675 us; the launch traced here: 672 us
  waiting for transfers between devices  540 us (80%)
  blocking collectives  57.2 us (8%)
  matrix products  43.5 us (6%)
  between operations  16.2 us (2%)
  other arithmetic  8.37 us (1%)
    reduce_scatter x1, waiting for transfers between devices, body(): lax.psum_scatter(partial_value, 'tensor', scatter_dimension=2, tiled=True)  117 us
    all_gather x1, waiting for transfers between devices, body(): merger_full = lax.all_gather(merger_w, 'dp', axis=0, tiled=True)  114 us
    reduce_scatter x1, waiting for transfers between devices, body(): lax.psum_scatter(merged_terms, 'tensor', scatter_dimension=1, tiled=True)  98.9 us
    all_gather x1, waiting for transfers between devices, body(): features = lax.all_gather(features_own, 'tensor', axis=2, tiled=True)  77.1 us
    all_gather x1, waiting for transfers between devices, body(): merged_all = lax.all_gather(merged, 'tensor', axis=1, tiled=True)  64.8 us
    psum x1, waiting for transfers between devices, body(): gradient = lax.psum(grad_pixels, 'group')  41.2 us
    all_gather x1, waiting for transfers between devices, body(): kv_gathered = lax.all_gather(kv_weight[0], 'dp', axis=1, tiled=True)  25.4 us
    psum x1, blocking collectives, body(): squares = lax.psum(jnp.sum(gradient * gradient, axis=(1, 2)), 'tensor')  20.7 us
  transfers between devices with their start and end apart: 7, of which 7 were waited for; matrix products, arithmetic and copies ran while one was open for 1% of the time, Pallas kernels for 0%

commit v1 on v0

v1 whole, which is shorter than its diff:
```python
import functools
import math

import jax
import jax.numpy as jnp
from jax import lax
from jax.experimental import pallas as pl
from jax.experimental.pallas import tpu as pltpu
from jax.sharding import PartitionSpec as P

F32 = jnp.float32
BF16 = jnp.bfloat16
NZ = 8
NT = 8
NY = 4
L = 128
MESH = pl.DeviceIdType.MESH


def dot(a, b):
    return jnp.dot(a, b, preferred_element_type=F32)


def dot_nt(a, b):
    return lax.dot_general(a, b, (((1,), (1,)), ((), ())), preferred_element_type=F32)


def kernel(
    ng,
    n_pixels,
    pix,
    patch_w,
    vgain,
    w_ref,
    gain_ref,
    kv_ref,
    q_ref,
    cot_ref,
    mask_ref,
    out_ref,
    wg,
    kvl,
    tok,
    hid,
    part1,
    s1,
    r1,
    ssq_s,
    ssq_r,
    kvpre,
    kvt,
    kvh,
    gkvh,
    gkv,
    scal,
    part4,
    s4,
    r4,
    xhat,
    gbuf,
    sqb,
    local_sem,
    zs,
    zr,
    xs,
    xr,
    as_,
    ar,
    rs1s,
    rs1r,
    sqs,
    sqr,
    ats,
    atr,
    bts,
    btr,
    ags,
    agr,
    scs,
    scr,
    rs4s,
    rs4r,
    grs,
    grr,
    fs,
    fr,
):
    g = lax.axis_index("group")
    d = lax.axis_index("dp")
    t = lax.axis_index("tensor")
    x, y = t // NY, lax.rem(t, NY)
    rows = w_ref.shape[0]
    half_rows = (rows + 2 * L) // 2
    slot = tok.shape[2]
    ntok = NZ * slot

    def zmod(i):
        return lax.rem(i + 2 * NZ, NZ)

    def cols(i):
        return pl.ds(pl.multiple_of(i * L, L), L)

    def remote(src, dst, send, recv, **to):
        return pltpu.make_async_remote_copy(
            src_ref=src, dst_ref=dst, send_sem=send, recv_sem=recv, device_id=to, device_id_type=MESH
        )

    sent = []

    def start(copy):
        copy.start()
        sent.append(copy)

    barrier = pltpu.get_barrier_semaphore()
    for r in range(1, NZ):
        pl.semaphore_signal(barrier, inc=1, device_id={"dp": zmod(d + r)}, device_id_type=MESH)
    for r in range(1, NT):
        pl.semaphore_signal(barrier, inc=1, device_id={"tensor": lax.rem(t + r, NT)}, device_id_type=MESH)
    for r in range(1, ng):
        pl.semaphore_signal(barrier, inc=1, device_id={"group": lax.rem(g + r, ng)}, device_id_type=MESH)

    own = [
        pltpu.make_async_copy(w_ref.at[:, cols(d)], wg.at[d, pl.ds(0, rows), cols(t)], local_sem.at[0])
    ]
    for k in range(2):
        own.append(
            pltpu.make_async_copy(
                kv_ref.at[k, cols(d), :], wg.at[d, pl.ds(rows + L * k, L), cols(t)], local_sem.at[1 + k]
            )
        )
    for c in own:
        c.start()
    pl.semaphore_wait(barrier, NZ - 1 + NT - 1 + ng - 1)

    def offset(p):
        return (p + 1) // 2 * (1 if p % 2 else -1)

    for c in own:
        c.wait()

    up = x * NY + lax.rem(y + 1, NY)
    down = x * NY + lax.rem(y + NY - 1, NY)
    far = x * NY + lax.rem(y + 2, NY)
    xo = (1 - x) * NY
    across = xo + y
    whole, lo, hi = (0, 2 * half_rows), (0, half_rows), (half_rows, half_rows)
    kinds = (
        (t, up, down, whole),
        (t, down, up, whole),
        (t, across, across, whole),
        (down, up, far, lo),
        (up, down, far, hi),
        (across, up, xo + lax.rem(y + NY - 1, NY), whole),
        (across, down, xo + lax.rem(y + 1, NY), whole),
        (far, across, xo + lax.rem(y + 2, NY), whole),
    )

    def plane(p):
        step = (p + 1) // 2
        return zmod(d + jnp.where(lax.rem(p, 2) == 1, step, -step))

    def xy(kind, p, incoming=False):
        block, to, arrives, (at, size) = kinds[kind]
        view = wg.at[plane(p), pl.ds(at, size), cols(arrives if incoming else block)]
        return remote(view, view, xs.at[kind, p], xr.at[kind, p], tensor=to)

    def z_in(p, which):
        at, size = ((0, rows), (rows, L), (rows + L, L))[which]
        view = wg.at[plane(p), pl.ds(at, size), cols(t)]
        return remote(view, view, zs.at[which, p], zr.at[which, p], dp=d)

    for kind in (0, 1, 2):
        xy(kind, jnp.int32(0)).start()
    for p in range(1, NZ):
        j = zmod(d - offset(p))
        start(
            remote(
                w_ref.at[:, cols(j)], wg.at[d, pl.ds(0, rows), cols(t)], zs.at[0, p], zr.at[0, p], dp=j
            )
        )
        for k in range(2):
            start(
                remote(
                    kv_ref.at[k, cols(j), :],
                    wg.at[d, pl.ds(rows + L * k, L), cols(t)],
                    zs.at[1 + k, p],
                    zr.at[1 + k, p],
                    dp=j,
                )
            )

    embed = dot(pix[...], patch_w[...])
    centered = embed - jnp.mean(embed, -1, keepdims=True)
    inv_dev = lax.rsqrt(jnp.mean(centered * centered, -1, keepdims=True) + 1e-06)
    normalized = centered * inv_dev
    xhat[...] = normalized
    visual = (normalized * vgain[...]).astype(BF16)
    for s in range(NZ):
        j, h = s // 2, s % 2
        tok[d, s] = visual[j * slot : (j + 1) * slot, h * rows : (h + 1) * rows]

    def ring_gather(buf, send, recv, halves):
        def block(src, k, side):
            if k < NZ // 2:
                return buf.at[src]
            return buf.at[src, pl.ds(side * halves, halves)]

        def go(k):
            for side, sign in ((0, 1), (1, -1)):
                view = block(zmod(d - sign * (k - 1)), k, side)
                start(remote(view, view, send.at[side, k - 1], recv.at[side, k - 1], dp=zmod(d + sign)))

        def arrive(k):
            for side, sign in ((0, 1), (1, -1)):
                view = block(zmod(d - sign * k), k, side)
                remote(view, view, send.at[side, k - 1], recv.at[side, k - 1], dp=zmod(d + sign)).wait_recv()

        return go, arrive

    go, arrive = ring_gather(tok, as_, ar, NZ // 2)
    go(1)
    hid[...] = jnp.zeros_like(hid)

    def piece(p):
        s = plane(p)
        hid[...] += dot(tok[:, s].reshape(ntok, rows), wg[s, :rows, :])
        for k in range(2):
            kvl[k, cols(s), :] = wg[s, pl.ds(rows + L * k, L), :]

    def weights_step(i, carry):
        @pl.when(jnp.logical_and(i >= 1, i < NZ))
        def _():
            for which in range(3):
                z_in(i, which).wait_recv()
            for kind in (0, 1, 2):
                xy(kind, i).start()

        @pl.when(jnp.logical_and(i >= 1, i < NZ + 1))
        def _():
            xy(0, i - 1, True).wait_recv()
            xy(3, i - 1).start()
            xy(1, i - 1, True).wait_recv()
            xy(4, i - 1).start()
            xy(2, i - 1, True).wait_recv()
            xy(5, i - 1).start()
            xy(6, i - 1).start()

        @pl.when(jnp.logical_and(i >= 2, i < NZ + 2))
        def _():
            xy(3, i - 2, True).wait_recv()
            xy(4, i - 2, True).wait_recv()
            xy(7, i - 2).start()

        @pl.when(i >= 3)
        def _():
            for kind in (5, 6, 7):
                xy(kind, i - 3, True).wait_recv()
            piece(i - 3)

        return carry

    lax.fori_loop(1, 2, weights_step, 0)
    arrive(1)
    go(2)
    lax.fori_loop(2, 3, weights_step, 0)
    arrive(2)
    go(3)
    arrive(3)
    go(4)
    arrive(4)
    lax.fori_loop(3, NZ + 3, weights_step, 0)

    hidden = hid[...].astype(BF16).astype(F32)
    hid[...] = hidden
    gain = jnp.concatenate(
        [gain_ref[:, pl.ds(pl.multiple_of((b * NZ + d) * L, L), L)] for b in range(NT)], axis=-1
    )
    total_sq = jnp.sum(hidden * hidden, -1, keepdims=True)
    ssq_s[...] = jnp.broadcast_to(total_sq, (ntok, L)).reshape(NZ, slot, L)
    for r in range(1, NZ):
        j = zmod(d + r)
        start(remote(ssq_s.at[j], ssq_r.at[d], sqs.at[r], sqr.at[r], dp=j))
    ssq_r[d] = ssq_s[d]
    scaled = (hidden * gain).astype(BF16)
    for k in range(2):
        part1[:, k] = dot(scaled, kvl[k]).reshape(NZ, slot, NT * L)

    def ring_sum(part, sbuf, rbuf, send, recv, chunks, n):
        def copy(k, c, side):
            sign = 1 - 2 * side
            if k == 1:
                at = pl.ds((2 * c + side) * n, n)
            else:
                at = pl.ds(2 * c * n, 2 * n)
            return remote(
                sbuf.at[side, k - 1, at],
                rbuf.at[side, k - 1, at],
                send.at[side, k - 1, c],
                recv.at[side, k - 1, c],
                dp=zmod(d + sign),
            )

        def step(k, c):
            for side in (0, 1):
                sign = 1 - 2 * side
                e = zmod(d + sign * (NZ // 2 + 1 - k))
                if k > 1:
                    copy(k - 1, c, side).wait_recv()
                for b in range(2):
                    at = pl.ds((2 * c + b) * n, n)
                    if k == 1 and b != side:
                        continue
                    value = part[e, at]
                    if k > 2 or (k == 2 and b == side):
                        value = value + rbuf[side, k - 2, at].astype(F32)
                    sbuf[side, k - 1, at] = value.astype(BF16)
                start(copy(k, c, side))

        def result(c):
            at = pl.ds(2 * c * n, 2 * n)
            value = part[d, at]
            for side in (0, 1):
                copy(NZ // 2, c, side).wait_recv()
                value = value + rbuf[side, NZ // 2 - 1, at].astype(F32)
            return value

        return step, result

    step, result = ring_sum(part1, s1, r1, rs1s, rs1r, 1, 1)
    for k in range(1, NZ // 2 + 1):
        step(k, 0)
    for r in range(1, NZ):
        j = zmod(d - r)
        remote(ssq_s.at[j], ssq_r.at[j], sqs.at[r], sqr.at[r], dp=j).wait_recv()
    width = gain_ref.shape[1]
    root = lax.rsqrt(jnp.sum(ssq_r[...], axis=0) / width + 1e-06)[:, :1]
    pre = result(0)
    kvpre[...] = pre
    kvt[...] = (pre * root).astype(BF16)

    for r in range(1, NT):
        j = lax.rem(t + r, NT)
        start(remote(kvt.at[:, :, cols(j)], kvh.at[t], ats.at[r], atr.at[r], tensor=j))
    kvh[t] = kvt[:, :, cols(t)]
    heads = q_ref.shape[1] // L
    query = jnp.concatenate([q_ref[:, h * L : (h + 1) * L] for h in range(heads)], axis=0)
    masked = (cot_ref[...].astype(F32) * mask_ref[...].astype(F32)).astype(BF16)
    grad_out = jnp.concatenate([masked[:, h * L : (h + 1) * L] for h in range(heads)], axis=0)
    for r in range(1, NT):
        j = lax.rem(t + NT - r, NT)
        remote(kvh.at[j], kvh.at[j], ats.at[r], atr.at[r], tensor=j).wait_recv()
    scale = 1.0 / math.sqrt(L)
    keys = kvh[:, 0].reshape(ntok, L)
    values = kvh[:, 1].reshape(ntok, L)
    scores = dot_nt(keys, query) * scale
    e = jnp.exp(scores - jnp.max(scores, axis=0, keepdims=True))
    probs = e / jnp.sum(e, axis=0, keepdims=True)
    grad_probs = dot_nt(values, grad_out)
    inner = jnp.sum(probs * grad_probs, axis=0, keepdims=True)
    grad_scores = (probs * (grad_probs - inner) * scale).astype(BF16)
    gkvh[:, 0] = dot(grad_scores, query).astype(BF16).reshape(NT, slot, L)
    gkvh[:, 1] = dot(probs.astype(BF16), grad_out).astype(BF16).reshape(NT, slot, L)
    for r in range(1, NT):
        j = lax.rem(t + r, NT)
        start(remote(gkvh.at[j], gkv.at[d, :, :, cols(t)], bts.at[r], btr.at[r], tensor=j))
    gkv[d, :, :, cols(t)] = gkvh[t]
    for r in range(1, NT):
        j = lax.rem(t + NT - r, NT)
        remote(gkvh.at[j], gkv.at[d, :, :, cols(j)], bts.at[r], btr.at[r], tensor=j).wait_recv()

    go, arrive = ring_gather(gkv, ags, agr, 1)
    go(1)
    products = gkv[d].astype(F32) * kvpre[...]
    row_sum = jnp.sum(products[0] + products[1], -1, keepdims=True)
    coef = root * root * root * row_sum / width
    lane = lax.broadcasted_iota(jnp.int32, (slot, L), 1)
    scal[d] = jnp.where(lane < L // 2, root, coef)
    for r in range(1, NZ):
        start(remote(scal.at[d], scal.at[d], scs.at[r], scr.at[r], dp=zmod(d + r)))
    for k in range(1, NZ // 2):
        arrive(k)
        go(k + 1)
    arrive(NZ // 2)
    for r in range(1, NZ):
        j = zmod(d - r)
        remote(scal.at[j], scal.at[j], scs.at[r], scr.at[r], dp=j).wait_recv()
    grad_feat = dot_nt(gkv[:, 0].reshape(ntok, NT * L), kvl[0]) + dot_nt(
        gkv[:, 1].reshape(ntok, NT * L), kvl[1]
    )
    both = scal[...].reshape(ntok, L)
    grad_hidden = (both[:, :1] * gain * grad_feat - hid[...] * both[:, L - 1 :]).astype(BF16)

    chunks = NZ // 2
    step, result = ring_sum(part4, s4, r4, rs4s, rs4r, chunks, 1)
    for c in range(chunks):
        for b in range(2):
            s = 2 * c + b
            part4[:, s] = dot_nt(grad_hidden, wg[s, :rows, :]).reshape(NZ, slot, rows)
        step(1, c)
    for k in range(2, NZ // 2 + 1):
        for c in range(chunks):
            step(k, c)
    blocks = []
    for c in range(chunks):
        value = result(c)
        blocks.append(jnp.concatenate([value[0], value[1]], axis=-1))
    grad_visual = jnp.concatenate(blocks, axis=0)

    gain_grad = grad_visual * vgain[...]
    normalized = xhat[...]
    embed_grad = (
        inv_dev
        * (
            gain_grad
            - jnp.mean(gain_grad, -1, keepdims=True)
            - normalized * jnp.mean(gain_grad * normalized, -1, keepdims=True)
        )
    ).astype(BF16)
    gbuf[g] = dot_nt(embed_grad, patch_w[...]).astype(BF16)
    for r in range(1, ng):
        start(remote(gbuf.at[g], gbuf.at[g], grs.at[r], grr.at[r], group=lax.rem(g + r, ng)))
    for r in range(1, ng):
        j = lax.rem(g + ng - r, ng)
        remote(gbuf.at[j], gbuf.at[j], grs.at[r], grr.at[r], group=j).wait_recv()
    gradient = gbuf[0].astype(F32)
    for m in range(1, ng):
        gradient = gradient + gbuf[m].astype(F32)
    sqb[t] = jnp.broadcast_to(jnp.sum(gradient * gradient), (8, L))
    for r in range(1, NT):
        start(remote(sqb.at[t], sqb.at[t], fs.at[r], fr.at[r], tensor=lax.rem(t + r, NT)))
    for r in range(1, NT):
        j = lax.rem(t + NT - r, NT)
        remote(sqb.at[j], sqb.at[j], fs.at[r], fr.at[r], tensor=j).wait_recv()
    squares = jnp.sum(sqb[...], axis=0)[:1, :1]
    out_ref[...] = jnp.tanh(gradient * lax.rsqrt(squares / n_pixels + 1e-06))

    for copy in sent:
        copy.wait_send()

    def drain(p, carry):
        for kind in range(8):
            xy(kind, p).wait_send()
        return carry

    lax.fori_loop(0, NZ, drain, 0)


def body(
    images,
    step_size,
    member_mask,
    patch_weight,
    vision_norm_gain,
    merger_weight,
    norm_gain,
    kv_weight,
    queries,
    cotangent,
    *,
    ng,
):
    patches, pixels = images.shape[1:]
    slot = patches // 4
    rows, width = merger_weight.shape[1:]
    vwidth = patch_weight.shape[2]
    half = NZ // 2
    turned = images[0].reshape(slot, 4, pixels).transpose(1, 0, 2).reshape(patches, pixels)
    dma = pltpu.SemaphoreType.DMA
    vmem = pl.BlockSpec(memory_space=pltpu.VMEM)
    direction = pl.pallas_call(
        functools.partial(kernel, ng, float(NT * patches * pixels)),
        out_shape=jax.ShapeDtypeStruct((patches, pixels), F32),
        in_specs=[vmem] * 9,
        out_specs=vmem,
        scratch_shapes=[
            pltpu.VMEM((NZ, rows + 2 * L, NT * L), BF16),
            pltpu.VMEM((2, NZ * L, NT * L), BF16),
            pltpu.VMEM((NZ, NZ, slot, rows), BF16),
            pltpu.VMEM((NZ * slot, NT * L), F32),
            pltpu.VMEM((NZ, 2, slot, NT * L), F32),
            pltpu.VMEM((2, half, 2, slot, NT * L), BF16),
            pltpu.VMEM((2, half, 2, slot, NT * L), BF16),
            pltpu.VMEM((NZ, slot, L), F32),
            pltpu.VMEM((NZ, slot, L), F32),
            pltpu.VMEM((2, slot, NT * L), F32),
            pltpu.VMEM((2, slot, NT * L), BF16),
            pltpu.VMEM((NT, 2, slot, L), BF16),
            pltpu.VMEM((NT, 2, slot, L), BF16),
            pltpu.VMEM((NZ, 2, slot, NT * L), BF16),
            pltpu.VMEM((NZ, slot, L), F32),
            pltpu.VMEM((NZ, NZ, slot, rows), F32),
            pltpu.VMEM((2, half, NZ, slot, rows), BF16),
            pltpu.VMEM((2, half, NZ, slot, rows), BF16),
            pltpu.VMEM((patches, vwidth), F32),
            pltpu.VMEM((ng, patches, pixels), BF16),
            pltpu.VMEM((NT, 8, L), F32),
            dma((3,)),
            dma((3, NZ)),
            dma((3, NZ)),
            dma((8, NZ)),
            dma((8, NZ)),
            dma((2, half)),
            dma((2, half)),
            dma((2, half, 1)),
            dma((2, half, 1)),
            dma((NZ,)),
            dma((NZ,)),
            dma((NT,)),
            dma((NT,)),
            dma((NT,)),
            dma((NT,)),
            dma((2, half)),
            dma((2, half)),
            dma((NZ,)),
            dma((NZ,)),
            dma((2, half, half)),
            dma((2, half, half)),
            dma((max(ng, 2),)),
            dma((max(ng, 2),)),
            dma((NT,)),
            dma((NT,)),
        ],
        compiler_params=pltpu.CompilerParams(
            collective_id=0, has_side_effects=True, vmem_limit_bytes=60 * 1024 * 1024
        ),
    )(
        turned.astype(BF16),
        patch_weight[0],
        vision_norm_gain,
        merger_weight[0],
        norm_gain,
        kv_weight[0],
        queries[0, 0],
        cotangent[0, 0],
        member_mask,
    )
    direction = direction.reshape(4, slot, pixels).transpose(1, 0, 2).reshape(images.shape)
    adversarial = jnp.clip(images + step_size[:, None, None] * direction, 0.0, 1.0)
    return adversarial, direction


def solution(mesh):
    placed = (
        P("dp", "tensor", None),
        P("dp"),
        P("group", "dp"),
        P("group", None, None),
        P("group", None),
        P("group", "dp", "tensor"),
        P("group", None),
        P("group", None, "dp", "tensor"),
        P("group", "dp", None, "tensor"),
        P("group", "dp", None, "tensor"),
    )
    return jax.shard_map(
        functools.partial(body, ng=mesh.shape["group"]),
        mesh=mesh,
        in_specs=placed,
        out_specs=(P("dp", "tensor", None), P("dp", "tensor", None)),
        check_vma=False,
    )
```

time: 675 us -> 249 us (0.37)
  waiting for transfers between devices: 540 us -> 0 us
  Pallas kernels: 0 us -> 241 us
  blocking collectives: 57.2 us -> 0 us
  matrix products: 43.5 us -> 0 us
  between operations: 16.2 us -> 1.99 us
  other arithmetic: 8.37 us -> 1.21 us
    all_gather x4 -> x0, waiting for transfers between devices: 281 us -> none  [the longest x1 114 us: body(): merger_full = lax.all_gather(merger_w, 'dp', axis=0, tiled=True)]
    pallas_call x0 -> x1, Pallas kernels: none -> 241 us  [body(): pl.pallas_call(functools.partial(kernel, ng, float(NT * patches * pixels)...]
    reduce_scatter x2 -> x0, waiting for transfers between devices: 216 us -> none  [the longest x1 117 us: body(): lax.psum_scatter(partial_value, 'tensor', scatter_dimension=2, tiled=True)]
    psum x3 -> x0, blocking collectives: 57.2 us -> none  [the longest x1 20.7 us: body(): squares = lax.psum(jnp.sum(gradient * gradient, axis=(1, 2)), 'tensor')]
    dot_general x8 -> x0, matrix products: 43.5 us -> none  [the longest x1 9.78 us: body(): jnp.einsum('itc,rc->itr', grad_hidden, merger_full, preferred_element_typ...]
    psum x1 -> x0, waiting for transfers between devices: 41.2 us -> none  [body(): gradient = lax.psum(grad_pixels, 'group')]
  transfers between devices with their start and end apart: 7 -> 0, of which waited for: 7 -> 0; matrix products, arithmetic and copies ran while one was open for 1% -> 0% of each run, Pallas kernels for 0% -> 0%
where the time goes in v1:
time: 249 us
  Pallas kernels  241 us (97%)
  local copies, waits for them, and re-layouts  4.19 us (2%)
    pallas_call x1, Pallas kernels, body(): pl.pallas_call(functools.partial(kernel, ng, float(NT * patches * pixels)...  241 us

profile of v1, /device:TPU:1, one launch (start us, length us, event | category | flops | bytes accessed | tf_op | source)
XLA Modules:
  0.0 248.9 jit_solution(16264139152584732869)
XLA Ops:
  0.6 1.2 convert_element_type.9
  1.8 0.2 copy.14
  2.0 0.1 convert_element_type.10
  2.0 0.7 copy.15
  3.4 241.5 %shard_map.113 = f32[128,588]{1,0:T(8,128)} custom-call(bf16[128,588]{1,0:T(8,128)(2,1)} %bitcast.17, bf16[588,1280]{1,0:T(8,128)(2,1)} %bitcast.13, f32[1,1280]{1,0:T(1,128)} %vgain.1, bf16[640,1024]{1,0:T(8,128)(2,1)} %bitcast.14, f32[1,8192]{1,0:T(1,128)} %gain_ref.1, bf16[2,1024,128]{2,1,0:T(8,128)(2,1)} %bitcast.19, bf16[32,1024]{1,0:T(8,128)(2,1)} %bitcast.20, ...), custom_call_target="tpu_custom_call" | custom-call | tf_op jit(solution)/shard_map/pallas_call | solution.py:470
  244.9 0.0 copy-start
  244.9 1.2 copy.21
  246.1 0.1 reshape.29
  246.2 0.0 copy-done
  246.2 0.2 copy.17
  247.1 0.9 copy.18
  248.0 0.9 copy.19
  (1 shorter events, 0.0 us)
Async XLA Ops:
  244.9 1.4 copy-start

commit v2 on v1

--- a/solution.py
+++ b/solution.py
@@ -14,6 +14,10 @@
 NT = 8
 NY = 4
 L = 128
+AHEAD = 3
+STOPS = (3, 5, 7, 8)
+LATE = 8
+PART = 192
 MESH = pl.DeviceIdType.MESH
 
 
@@ -132,9 +136,6 @@
         c.start()
     pl.semaphore_wait(barrier, NZ - 1 + NT - 1 + ng - 1)
 
-    def offset(p):
-        return (p + 1) // 2 * (1 if p % 2 else -1)
-
     for c in own:
         c.wait()
 
@@ -144,15 +145,18 @@
     xo = (1 - x) * NY
     across = xo + y
     whole, lo, hi = (0, 2 * half_rows), (0, half_rows), (half_rows, half_rows)
+    first, rest = (0, PART), (PART, 2 * half_rows - PART)
     kinds = (
         (t, up, down, whole),
         (t, down, up, whole),
         (t, across, across, whole),
         (down, up, far, lo),
         (up, down, far, hi),
-        (across, up, xo + lax.rem(y + NY - 1, NY), whole),
-        (across, down, xo + lax.rem(y + 1, NY), whole),
+        (across, up, xo + lax.rem(y + NY - 1, NY), rest),
+        (across, down, xo + lax.rem(y + 1, NY), rest),
         (far, across, xo + lax.rem(y + 2, NY), whole),
+        (up, across, xo + lax.rem(y + 1, NY), first),
+        (down, across, xo + lax.rem(y + NY - 1, NY), first),
     )
 
     def plane(p):
@@ -169,25 +173,19 @@
         view = wg.at[plane(p), pl.ds(at, size), cols(t)]
         return remote(view, view, zs.at[which, p], zr.at[which, p], dp=d)
 
+    def z_out(p, which):
+        step = (p + 1) // 2
+        j = zmod(d + jnp.where(lax.rem(p, 2) == 1, -step, step))
+        at, size = ((0, rows), (rows, L), (rows + L, L))[which]
+        src = w_ref.at[:, cols(j)] if which == 0 else kv_ref.at[which - 1, cols(j), :]
+        dst = wg.at[d, pl.ds(at, size), cols(t)]
+        return remote(src, dst, zs.at[which, p], zr.at[which, p], dp=j)
+
     for kind in (0, 1, 2):
         xy(kind, jnp.int32(0)).start()
-    for p in range(1, NZ):
-        j = zmod(d - offset(p))
-        start(
-            remote(
-                w_ref.at[:, cols(j)], wg.at[d, pl.ds(0, rows), cols(t)], zs.at[0, p], zr.at[0, p], dp=j
-            )
-        )
-        for k in range(2):
-            start(
-                remote(
-                    kv_ref.at[k, cols(j), :],
-                    wg.at[d, pl.ds(rows + L * k, L), cols(t)],
-                    zs.at[1 + k, p],
-                    zr.at[1 + k, p],
-                    dp=j,
-                )
-            )
+    for p in range(1, AHEAD + 1):
+        for which in range(3):
+            z_out(jnp.int32(p), which).start()
 
     embed = dot(pix[...], patch_w[...])
     centered = embed - jnp.mean(embed, -1, keepdims=True)
@@ -235,12 +233,19 @@
             for kind in (0, 1, 2):
                 xy(kind, i).start()
 
+        @pl.when(i + AHEAD < NZ)
+        def _():
+            for which in range(3):
+                z_out(i + AHEAD, which).start()
+
         @pl.when(jnp.logical_and(i >= 1, i < NZ + 1))
         def _():
             xy(0, i - 1, True).wait_recv()
             xy(3, i - 1).start()
+            xy(9, i - 1).start()
             xy(1, i - 1, True).wait_recv()
             xy(4, i - 1).start()
+            xy(8, i - 1).start()
             xy(2, i - 1, True).wait_recv()
             xy(5, i - 1).start()
             xy(6, i - 1).start()
@@ -253,22 +258,24 @@
 
         @pl.when(i >= 3)
         def _():
-            for kind in (5, 6, 7):
+            for kind in (5, 6, 7, 8, 9):
                 xy(kind, i - 3, True).wait_recv()
-            piece(i - 3)
+
+        @pl.when(i >= LATE)
+        def _():
+            piece(i - LATE)
 
         return carry
 
-    lax.fori_loop(1, 2, weights_step, 0)
-    arrive(1)
-    go(2)
-    lax.fori_loop(2, 3, weights_step, 0)
-    arrive(2)
-    go(3)
-    arrive(3)
-    go(4)
-    arrive(4)
-    lax.fori_loop(3, NZ + 3, weights_step, 0)
+    at = 1
+    for k, stop in enumerate(STOPS):
+        lax.fori_loop(at, stop, weights_step, 0)
+        arrive(k + 1)
+        if k < 3:
+            go(k + 2)
+        at = stop
+    lax.fori_loop(at, NZ + 3, weights_step, 0)
+    lax.fori_loop(NZ + 3 - LATE, NZ, lambda p, carry: (piece(p), carry)[1], 0)
 
     hidden = hid[...].astype(BF16).astype(F32)
     hid[...] = hidden
@@ -438,8 +445,14 @@
         copy.wait_send()
 
     def drain(p, carry):
-        for kind in range(8):
+        for kind in range(len(kinds)):
             xy(kind, p).wait_send()
+
+        @pl.when(p > 0)
+        def _():
+            for which in range(3):
+                z_out(p, which).wait_send()
+
         return carry
 
     lax.fori_loop(0, NZ, drain, 0)
@@ -497,8 +510,8 @@
             dma((3,)),
             dma((3, NZ)),
             dma((3, NZ)),
-            dma((8, NZ)),
-            dma((8, NZ)),
+            dma((10, NZ)),
+            dma((10, NZ)),
             dma((2, half)),
             dma((2, half)),
             dma((2, half, 1)),

time: 249 us -> 213 us (0.86)
  Pallas kernels: 241 us -> 205 us
    pallas_call x1, Pallas kernels: 241 us -> 205 us  [body(): pl.pallas_call(functools.partial(kernel, ng, float(NT * patches * pixels)...]
where the time goes in v2:
time: 213 us; the launch traced here: 212 us
  Pallas kernels  205 us (96%)
  local copies, waits for them, and re-layouts  4.19 us (2%)
    pallas_call x1, Pallas kernels, body(): pl.pallas_call(functools.partial(kernel, ng, float(NT * patches * pixels)...  205 us

profile of v2, /device:TPU:1, one launch (start us, length us, event | category | flops | bytes accessed | tf_op | source)
XLA Modules:
  0.0 212.3 jit_solution(9373299050364527133)
XLA Ops:
  0.6 1.2 convert_element_type.9
  1.8 0.2 copy.14
  2.0 0.1 convert_element_type.10
  2.0 0.7 copy.15
  3.4 204.9 %shard_map.113 = f32[128,588]{1,0:T(8,128)} custom-call(bf16[128,588]{1,0:T(8,128)(2,1)} %bitcast.17, bf16[588,1280]{1,0:T(8,128)(2,1)} %bitcast.13, f32[1,1280]{1,0:T(1,128)} %vgain.1, bf16[640,1024]{1,0:T(8,128)(2,1)} %bitcast.14, f32[1,8192]{1,0:T(1,128)} %gain_ref.1, bf16[2,1024,128]{2,1,0:T(8,128)(2,1)} %bitcast.19, bf16[32,1024]{1,0:T(8,128)(2,1)} %bitcast.20, ...), custom_call_target="tpu_custom_call" | custom-call | tf_op jit(solution)/shard_map/pallas_call | solution.py:483
  208.3 0.0 copy-start
  208.4 1.2 copy.21
  209.6 0.1 reshape.29
  209.7 0.0 copy-done
  209.7 0.2 copy.17
  210.6 0.9 copy.18
  211.5 0.9 copy.19
  (1 shorter events, 0.0 us)
Async XLA Ops:
  208.3 1.4 copy-start

commit v3 on v2

--- a/solution.py
+++ b/solution.py
@@ -16,7 +16,6 @@
 L = 128
 AHEAD = 3
 STOPS = (3, 5, 7, 8)
-LATE = 8
 PART = 192
 MESH = pl.DeviceIdType.MESH
 
@@ -33,7 +32,7 @@
     ng,
     n_pixels,
     pix,
-    patch_w,
+    patch_hbm,
     vgain,
     w_ref,
     gain_ref,
@@ -63,6 +62,7 @@
     xhat,
     gbuf,
     sqb,
+    patch_w,
     local_sem,
     zs,
     zr,
@@ -115,6 +115,8 @@
         copy.start()
         sent.append(copy)
 
+    load_patch = pltpu.make_async_copy(patch_hbm, patch_w, local_sem.at[3])
+    load_patch.start()
     barrier = pltpu.get_barrier_semaphore()
     for r in range(1, NZ):
         pl.semaphore_signal(barrier, inc=1, device_id={"dp": zmod(d + r)}, device_id_type=MESH)
@@ -187,6 +189,7 @@
         for which in range(3):
             z_out(jnp.int32(p), which).start()
 
+    load_patch.wait()
     embed = dot(pix[...], patch_w[...])
     centered = embed - jnp.mean(embed, -1, keepdims=True)
     inv_dev = lax.rsqrt(jnp.mean(centered * centered, -1, keepdims=True) + 1e-06)
@@ -197,33 +200,48 @@
         j, h = s // 2, s % 2
         tok[d, s] = visual[j * slot : (j + 1) * slot, h * rows : (h + 1) * rows]
 
-    def ring_gather(buf, send, recv, halves):
-        def block(src, k, side):
-            if k < NZ // 2:
-                return buf.at[src]
-            return buf.at[src, pl.ds(side * halves, halves)]
+    def ring_gather(buf, send, recv, views):
+        n = len(views)
+
+        def copy(src, k, side, c):
+            view = buf.at[(src,) + views[c]]
+            to = zmod(d + 1 - 2 * side)
+            return remote(view, view, send.at[side, k - 1, c], recv.at[side, k - 1, c], dp=to)
+
+        def order(k, side):
+            own_half = list(range(side * n // 2, (side + 1) * n // 2))
+            return own_half if k == NZ // 2 else own_half + [c for c in range(n) if c not in own_half]
 
         def go(k):
-            for side, sign in ((0, 1), (1, -1)):
-                view = block(zmod(d - sign * (k - 1)), k, side)
-                start(remote(view, view, send.at[side, k - 1], recv.at[side, k - 1], dp=zmod(d + sign)))
-
-        def arrive(k):
-            for side, sign in ((0, 1), (1, -1)):
-                view = block(zmod(d - sign * k), k, side)
-                remote(view, view, send.at[side, k - 1], recv.at[side, k - 1], dp=zmod(d + sign)).wait_recv()
+            for i in range(n):
+                for side in (0, 1):
+                    if i < len(order(k, side)):
+                        start(copy(zmod(d - (1 - 2 * side) * (k - 1)), k, side, order(k, side)[i]))
+
+        def arrive(k, then_go=False):
+            for i in range(n):
+                for side in (0, 1):
+                    if i < len(order(k, side)):
+                        src, c = zmod(d - (1 - 2 * side) * k), order(k, side)[i]
+                        copy(src, k, side, c).wait_recv()
+                        if then_go and c in order(k + 1, side):
+                            start(copy(src, k + 1, side, c))
 
         return go, arrive
 
-    go, arrive = ring_gather(tok, as_, ar, NZ // 2)
+    go, arrive = ring_gather(tok, as_, ar, [(pl.ds(0, NZ // 2),), (pl.ds(NZ // 2, NZ // 2),)])
     go(1)
     hid[...] = jnp.zeros_like(hid)
 
-    def piece(p):
+    def piece(p, carry):
         s = plane(p)
         hid[...] += dot(tok[:, s].reshape(ntok, rows), wg[s, :rows, :])
         for k in range(2):
             kvl[k, cols(s), :] = wg[s, pl.ds(rows + L * k, L), :]
+        return carry
+
+    def pieces(start_at, stop_at):
+        lax.fori_loop(start_at, stop_at, piece, 0)
 
     def weights_step(i, carry):
         @pl.when(jnp.logical_and(i >= 1, i < NZ))
@@ -256,26 +274,25 @@
             xy(4, i - 2, True).wait_recv()
             xy(7, i - 2).start()
 
+        @pl.when(i >= NZ)
+        def _():
+            first_piece = 3 * (i - NZ)
+            pieces(first_piece, jnp.minimum(first_piece + 3, NZ - 1))
+
         @pl.when(i >= 3)
         def _():
             for kind in (5, 6, 7, 8, 9):
                 xy(kind, i - 3, True).wait_recv()
 
-        @pl.when(i >= LATE)
-        def _():
-            piece(i - LATE)
-
         return carry
 
     at = 1
     for k, stop in enumerate(STOPS):
         lax.fori_loop(at, stop, weights_step, 0)
-        arrive(k + 1)
-        if k < 3:
-            go(k + 2)
+        arrive(k + 1, k < 3)
         at = stop
     lax.fori_loop(at, NZ + 3, weights_step, 0)
-    lax.fori_loop(NZ + 3 - LATE, NZ, lambda p, carry: (piece(p), carry)[1], 0)
+    pieces(NZ - 1, NZ)
 
     hidden = hid[...].astype(BF16).astype(F32)
     hid[...] = hidden
@@ -289,9 +306,6 @@
         start(remote(ssq_s.at[j], ssq_r.at[d], sqs.at[r], sqr.at[r], dp=j))
     ssq_r[d] = ssq_s[d]
     scaled = (hidden * gain).astype(BF16)
-    for k in range(2):
-        part1[:, k] = dot(scaled, kvl[k]).reshape(NZ, slot, NT * L)
-
     def ring_sum(part, sbuf, rbuf, send, recv, chunks, n):
         def copy(k, c, side):
             sign = 1 - 2 * side
@@ -333,17 +347,28 @@
 
         return step, result
 
-    step, result = ring_sum(part1, s1, r1, rs1s, rs1r, 1, 1)
-    for k in range(1, NZ // 2 + 1):
-        step(k, 0)
+    chunks = NZ // 2
+    step, result = ring_sum(part1, s1, r1, rs1s, rs1r, chunks, 1)
+    for c in range(chunks):
+        at = c % 2 * 4 * L
+        share = dot(scaled, kvl[c // 2, :, at : at + 4 * L])
+        for b in range(2):
+            part1[:, 2 * c + b] = share[:, 2 * b * L : 2 * (b + 1) * L].reshape(NZ, slot, 2 * L)
+        step(1, c)
+    for k in range(2, NZ // 2 + 1):
+        for c in range(chunks):
+            step(k, c)
     for r in range(1, NZ):
         j = zmod(d - r)
         remote(ssq_s.at[j], ssq_r.at[j], sqs.at[r], sqr.at[r], dp=j).wait_recv()
     width = gain_ref.shape[1]
     root = lax.rsqrt(jnp.sum(ssq_r[...], axis=0) / width + 1e-06)[:, :1]
-    pre = result(0)
-    kvpre[...] = pre
-    kvt[...] = (pre * root).astype(BF16)
+    for c in range(chunks):
+        pre = result(c)
+        for b in range(2):
+            at = (c % 2 * 2 + b) * 2 * L
+            kvpre[c // 2, :, at : at + 2 * L] = pre[b]
+            kvt[c // 2, :, at : at + 2 * L] = (pre[b] * root).astype(BF16)
 
     for r in range(1, NT):
         j = lax.rem(t + r, NT)
@@ -375,7 +400,8 @@
         j = lax.rem(t + NT - r, NT)
         remote(gkvh.at[j], gkv.at[d, :, :, cols(j)], bts.at[r], btr.at[r], tensor=j).wait_recv()
 
-    go, arrive = ring_gather(gkv, ags, agr, 1)
+    spans = [(k, slice(None), pl.ds(h * 4 * L, 4 * L)) for k in range(2) for h in range(2)]
+    go, arrive = ring_gather(gkv, ags, agr, spans)
     go(1)
     products = gkv[d].astype(F32) * kvpre[...]
     row_sum = jnp.sum(products[0] + products[1], -1, keepdims=True)
@@ -385,8 +411,7 @@
     for r in range(1, NZ):
         start(remote(scal.at[d], scal.at[d], scs.at[r], scr.at[r], dp=zmod(d + r)))
     for k in range(1, NZ // 2):
-        arrive(k)
-        go(k + 1)
+        arrive(k, True)
     arrive(NZ // 2)
     for r in range(1, NZ):
         j = zmod(d - r)
@@ -397,7 +422,6 @@
     both = scal[...].reshape(ntok, L)
     grad_hidden = (both[:, :1] * gain * grad_feat - hid[...] * both[:, L - 1 :]).astype(BF16)
 
-    chunks = NZ // 2
     step, result = ring_sum(part4, s4, r4, rs4s, rs4r, chunks, 1)
     for c in range(chunks):
         for b in range(2):
@@ -480,19 +504,20 @@
     turned = images[0].reshape(slot, 4, pixels).transpose(1, 0, 2).reshape(patches, pixels)
     dma = pltpu.SemaphoreType.DMA
     vmem = pl.BlockSpec(memory_space=pltpu.VMEM)
+    anywhere = pl.BlockSpec(memory_space=pl.ANY)
     direction = pl.pallas_call(
         functools.partial(kernel, ng, float(NT * patches * pixels)),
         out_shape=jax.ShapeDtypeStruct((patches, pixels), F32),
-        in_specs=[vmem] * 9,
+        in_specs=[vmem, anywhere, vmem, anywhere, vmem, anywhere, vmem, vmem, vmem],
         out_specs=vmem,
         scratch_shapes=[
             pltpu.VMEM((NZ, rows + 2 * L, NT * L), BF16),
             pltpu.VMEM((2, NZ * L, NT * L), BF16),
             pltpu.VMEM((NZ, NZ, slot, rows), BF16),
             pltpu.VMEM((NZ * slot, NT * L), F32),
-            pltpu.VMEM((NZ, 2, slot, NT * L), F32),
-            pltpu.VMEM((2, half, 2, slot, NT * L), BF16),
-            pltpu.VMEM((2, half, 2, slot, NT * L), BF16),
+            pltpu.VMEM((NZ, NZ, slot, 2 * L), F32),
+            pltpu.VMEM((2, half, NZ, slot, 2 * L), BF16),
+            pltpu.VMEM((2, half, NZ, slot, 2 * L), BF16),
             pltpu.VMEM((NZ, slot, L), F32),
             pltpu.VMEM((NZ, slot, L), F32),
             pltpu.VMEM((2, slot, NT * L), F32),
@@ -507,23 +532,24 @@
             pltpu.VMEM((patches, vwidth), F32),
             pltpu.VMEM((ng, patches, pixels), BF16),
             pltpu.VMEM((NT, 8, L), F32),
-            dma((3,)),
+            pltpu.VMEM((pixels, vwidth), BF16),
+            dma((4,)),
             dma((3, NZ)),
             dma((3, NZ)),
             dma((10, NZ)),
             dma((10, NZ)),
-            dma((2, half)),
-            dma((2, half)),
-            dma((2, half, 1)),
-            dma((2, half, 1)),
+            dma((2, half, 2)),
+            dma((2, half, 2)),
+            dma((2, half, half)),
+            dma((2, half, half)),
             dma((NZ,)),
             dma((NZ,)),
             dma((NT,)),
             dma((NT,)),
             dma((NT,)),
             dma((NT,)),
-            dma((2, half)),
-            dma((2, half)),
+            dma((2, half, half)),
+            dma((2, half, half)),
             dma((NZ,)),
             dma((NZ,)),
             dma((2, half, half)),

time: 213 us -> 201 us (0.944)
  Pallas kernels: 205 us -> 193 us
    pallas_call x1, Pallas kernels: 205 us -> 193 us  [body(): pl.pallas_call(functools.partial(kernel, ng, float(NT * patches * pixels)...]
where the time goes in v3:
time: 201 us; the launch traced here: 200 us
  Pallas kernels  193 us (96%)
  local copies, waits for them, and re-layouts  4.19 us (2%)
    pallas_call x1, Pallas kernels, body(): pl.pallas_call(functools.partial(kernel, ng, float(NT * patches * pixels)...  193 us

profile of v3, /device:TPU:1, one launch (start us, length us, event | category | flops | bytes accessed | tf_op | source)
XLA Modules:
  0.0 200.5 jit_solution(7519816903745965453)
XLA Ops:
  0.6 1.2 convert_element_type.9
  1.8 0.2 copy.14
  2.0 0.1 convert_element_type.10
  2.0 0.7 copy.15
  3.4 193.1 %shard_map.113 = f32[128,588]{1,0:T(8,128)} custom-call(bf16[128,588]{1,0:T(8,128)(2,1)} %bitcast.17, bf16[588,1280]{1,0:T(8,128)(2,1)} %bitcast.13, f32[1,1280]{1,0:T(1,128)} %vgain.1, bf16[640,1024]{1,0:T(8,128)(2,1)} %bitcast.14, f32[1,8192]{1,0:T(1,128)} %gain_ref.1, bf16[2,1024,128]{2,1,0:T(8,128)(2,1)} %bitcast.19, bf16[32,1024]{1,0:T(8,128)(2,1)} %bitcast.20, ...), custom_call_target="tpu_custom_call" | custom-call | tf_op jit(solution)/shard_map/pallas_call | solution.py:508
  196.5 0.0 copy-start
  196.5 1.2 copy.21
  197.7 0.1 reshape.29
  197.8 0.0 copy-done
  197.9 0.2 copy.17
  198.7 0.9 copy.18
  199.6 0.9 copy.19
  (1 shorter events, 0.0 us)
Async XLA Ops:
  196.5 1.4 copy-start

commit v4 on v3

--- a/solution.py
+++ b/solution.py
@@ -16,7 +16,6 @@
 L = 128
 AHEAD = 3
 STOPS = (3, 5, 7, 8)
-PART = 192
 MESH = pl.DeviceIdType.MESH
 
 
@@ -31,7 +30,7 @@
 def kernel(
     ng,
     n_pixels,
-    pix,
+    pix_hbm,
     patch_hbm,
     vgain,
     w_ref,
@@ -40,7 +39,9 @@
     q_ref,
     cot_ref,
     mask_ref,
-    out_ref,
+    step_ref,
+    adv_hbm,
+    dir_hbm,
     wg,
     kvl,
     tok,
@@ -63,6 +64,10 @@
     gbuf,
     sqb,
     patch_w,
+    heads_in,
+    pix,
+    adv_ref,
+    dir_ref,
     local_sem,
     zs,
     zr,
@@ -94,7 +99,6 @@
     t = lax.axis_index("tensor")
     x, y = t // NY, lax.rem(t, NY)
     rows = w_ref.shape[0]
-    half_rows = (rows + 2 * L) // 2
     slot = tok.shape[2]
     ntok = NZ * slot
 
@@ -117,6 +121,8 @@
 
     load_patch = pltpu.make_async_copy(patch_hbm, patch_w, local_sem.at[3])
     load_patch.start()
+    load_pixels = pltpu.make_async_copy(pix_hbm.at[:, 0, :], pix, local_sem.at[4])
+    load_pixels.start()
     barrier = pltpu.get_barrier_semaphore()
     for r in range(1, NZ):
         pl.semaphore_signal(barrier, inc=1, device_id={"dp": zmod(d + r)}, device_id_type=MESH)
@@ -125,72 +131,105 @@
     for r in range(1, ng):
         pl.semaphore_signal(barrier, inc=1, device_id={"group": lax.rem(g + r, ng)}, device_id_type=MESH)
 
-    own = [
-        pltpu.make_async_copy(w_ref.at[:, cols(d)], wg.at[d, pl.ds(0, rows), cols(t)], local_sem.at[0])
-    ]
+    own = [pltpu.make_async_copy(w_ref.at[:, cols(d)], wg.at[d, :, cols(t)], local_sem.at[0])]
     for k in range(2):
         own.append(
-            pltpu.make_async_copy(
-                kv_ref.at[k, cols(d), :], wg.at[d, pl.ds(rows + L * k, L), cols(t)], local_sem.at[1 + k]
-            )
+            pltpu.make_async_copy(kv_ref.at[k, cols(d), :], kvl.at[k, cols(d), cols(t)], local_sem.at[1 + k])
         )
     for c in own:
         c.start()
     pl.semaphore_wait(barrier, NZ - 1 + NT - 1 + ng - 1)
-
-    for c in own:
-        c.wait()
 
     up = x * NY + lax.rem(y + 1, NY)
     down = x * NY + lax.rem(y + NY - 1, NY)
     far = x * NY + lax.rem(y + 2, NY)
     xo = (1 - x) * NY
     across = xo + y
-    whole, lo, hi = (0, 2 * half_rows), (0, half_rows), (half_rows, half_rows)
-    first, rest = (0, PART), (PART, 2 * half_rows - PART)
-    kinds = (
-        (t, up, down, whole),
-        (t, down, up, whole),
-        (t, across, across, whole),
-        (down, up, far, lo),
-        (up, down, far, hi),
-        (across, up, xo + lax.rem(y + NY - 1, NY), rest),
-        (across, down, xo + lax.rem(y + 1, NY), rest),
-        (far, across, xo + lax.rem(y + 2, NY), whole),
-        (up, across, xo + lax.rem(y + 1, NY), first),
-        (down, across, xo + lax.rem(y + NY - 1, NY), first),
-    )
+    def kinds(height):
+        part = height // 6 // 16 * 16
+        whole, lo, hi = (0, height), (0, height // 2), (height // 2, height // 2)
+        first, rest = (0, part), (part, height - part)
+        return (
+            (t, up, down, whole),
+            (t, down, up, whole),
+            (t, across, across, whole),
+            (down, up, far, lo),
+            (up, down, far, hi),
+            (across, up, xo + lax.rem(y + NY - 1, NY), rest),
+            (across, down, xo + lax.rem(y + 1, NY), rest),
+            (far, across, xo + lax.rem(y + 2, NY), whole),
+            (up, across, xo + lax.rem(y + 1, NY), first),
+            (down, across, xo + lax.rem(y + NY - 1, NY), first),
+        )
 
     def plane(p):
         step = (p + 1) // 2
         return zmod(d + jnp.where(lax.rem(p, 2) == 1, step, -step))
 
+    def is_kv(p):
+        return isinstance(p, int) and p >= NZ
+
     def xy(kind, p, incoming=False):
-        block, to, arrives, (at, size) = kinds[kind]
-        view = wg.at[plane(p), pl.ds(at, size), cols(arrives if incoming else block)]
-        return remote(view, view, xs.at[kind, p], xr.at[kind, p], tensor=to)
-
-    def z_in(p, which):
-        at, size = ((0, rows), (rows, L), (rows + L, L))[which]
-        view = wg.at[plane(p), pl.ds(at, size), cols(t)]
-        return remote(view, view, zs.at[which, p], zr.at[which, p], dp=d)
-
-    def z_out(p, which):
+        buf = kvl.at[p - NZ] if is_kv(p) else wg.at[plane(jnp.int32(p))]
+        block, to, arrives, (at, size) = kinds(buf.shape[0])[kind]
+        view = buf.at[pl.ds(at, size), cols(arrives if incoming else block)]
+        src = w_ref.at[:, cols(d)] if isinstance(p, int) and p == 0 and kind < 3 and not incoming else view
+        return remote(src, view, xs.at[kind, p], xr.at[kind, p], tensor=to)
+
+    def z_copy(p, which, incoming=False):
         step = (p + 1) // 2
         j = zmod(d + jnp.where(lax.rem(p, 2) == 1, -step, step))
-        at, size = ((0, rows), (rows, L), (rows + L, L))[which]
-        src = w_ref.at[:, cols(j)] if which == 0 else kv_ref.at[which - 1, cols(j), :]
-        dst = wg.at[d, pl.ds(at, size), cols(t)]
+        home = plane(p) if incoming else d
+        if which == 0:
+            src, dst = w_ref.at[:, cols(j)], wg.at[home, :, cols(t)]
+        else:
+            src, dst = kv_ref.at[which - 1, cols(j), :], kvl.at[which - 1, cols(home), cols(t)]
         return remote(src, dst, zs.at[which, p], zr.at[which, p], dp=j)
 
+    def stage_a(p):
+        if is_kv(p):
+            for other in range(1, NZ):
+                z_copy(jnp.int32(other), p - NZ + 1, True).wait_recv()
+        else:
+            z_copy(p, 0, True).wait_recv()
+        for kind in (0, 1, 2):
+            xy(kind, p).start()
+
+    def stage_b(p):
+        xy(0, p, True).wait_recv()
+        xy(3, p).start()
+        xy(9, p).start()
+        xy(1, p, True).wait_recv()
+        xy(4, p).start()
+        xy(8, p).start()
+        xy(2, p, True).wait_recv()
+        xy(5, p).start()
+        xy(6, p).start()
+
+    def stage_c(p):
+        xy(3, p, True).wait_recv()
+        xy(4, p, True).wait_recv()
+        xy(7, p).start()
+
+    def stage_d(p):
+        for kind in (5, 6, 7, 8, 9):
+            xy(kind, p, True).wait_recv()
+
     for kind in (0, 1, 2):
-        xy(kind, jnp.int32(0)).start()
+        xy(kind, 0).start()
     for p in range(1, AHEAD + 1):
-        for which in range(3):
-            z_out(jnp.int32(p), which).start()
-
+        z_copy(jnp.int32(p), 0).start()
+
+    patches = pix.shape[1]
+    natural = lax.broadcasted_iota(jnp.int32, (patches, patches), 0)
+    turned = lax.broadcasted_iota(jnp.int32, (patches, patches), 1)
+    per = patches // slot
+    swap = jnp.where(turned == lax.rem(natural, per) * slot + natural // per, 1.0, 0.0).astype(BF16)
+    back = jnp.where(natural == lax.rem(turned, per) * slot + turned // per, 1.0, 0.0).astype(BF16)
+    load_pixels.wait()
+    pixels = dot_nt(back, pix[...].astype(BF16)).astype(BF16)
     load_patch.wait()
-    embed = dot(pix[...], patch_w[...])
+    embed = dot(pixels, patch_w[...])
     centered = embed - jnp.mean(embed, -1, keepdims=True)
     inv_dev = lax.rsqrt(jnp.mean(centered * centered, -1, keepdims=True) + 1e-06)
     normalized = centered * inv_dev
@@ -231,58 +270,38 @@
 
     go, arrive = ring_gather(tok, as_, ar, [(pl.ds(0, NZ // 2),), (pl.ds(NZ // 2, NZ // 2),)])
     go(1)
+    heads = q_ref.shape[1] // L
+    heads_in[0] = jnp.concatenate([q_ref[:, h * L : (h + 1) * L] for h in range(heads)], axis=0)
+    masked = (cot_ref[...].astype(F32) * mask_ref[...].astype(F32)).astype(BF16)
+    heads_in[1] = jnp.concatenate([masked[:, h * L : (h + 1) * L] for h in range(heads)], axis=0)
     hid[...] = jnp.zeros_like(hid)
+    for c in own:
+        c.wait()
 
     def piece(p, carry):
         s = plane(p)
-        hid[...] += dot(tok[:, s].reshape(ntok, rows), wg[s, :rows, :])
-        for k in range(2):
-            kvl[k, cols(s), :] = wg[s, pl.ds(rows + L * k, L), :]
+        hid[...] += dot(tok[:, s].reshape(ntok, rows), wg[s])
         return carry
 
     def pieces(start_at, stop_at):
         lax.fori_loop(start_at, stop_at, piece, 0)
 
     def weights_step(i, carry):
-        @pl.when(jnp.logical_and(i >= 1, i < NZ))
-        def _():
-            for which in range(3):
-                z_in(i, which).wait_recv()
-            for kind in (0, 1, 2):
-                xy(kind, i).start()
+        stage_a(i)
 
         @pl.when(i + AHEAD < NZ)
         def _():
-            for which in range(3):
-                z_out(i + AHEAD, which).start()
-
-        @pl.when(jnp.logical_and(i >= 1, i < NZ + 1))
+            z_copy(i + AHEAD, 0).start()
+
+        stage_b(i - 1)
+
+        @pl.when(i >= 2)
         def _():
-            xy(0, i - 1, True).wait_recv()
-            xy(3, i - 1).start()
-            xy(9, i - 1).start()
-            xy(1, i - 1, True).wait_recv()
-            xy(4, i - 1).start()
-            xy(8, i - 1).start()
-            xy(2, i - 1, True).wait_recv()
-            xy(5, i - 1).start()
-            xy(6, i - 1).start()
-
-        @pl.when(jnp.logical_and(i >= 2, i < NZ + 2))
-        def _():
-            xy(3, i - 2, True).wait_recv()
-            xy(4, i - 2, True).wait_recv()
-            xy(7, i - 2).start()
-
-        @pl.when(i >= NZ)
-        def _():
-            first_piece = 3 * (i - NZ)
-            pieces(first_piece, jnp.minimum(first_piece + 3, NZ - 1))
+            stage_c(i - 2)
 
         @pl.when(i >= 3)
         def _():
-            for kind in (5, 6, 7, 8, 9):
-                xy(kind, i - 3, True).wait_recv()
+            stage_d(i - 3)
 
         return carry
 
@@ -290,9 +309,26 @@
     for k, stop in enumerate(STOPS):
         lax.fori_loop(at, stop, weights_step, 0)
         arrive(k + 1, k < 3)
+        if k in (1, 2):
+            for p in range(1, NZ):
+                start(z_copy(jnp.int32(p), k))
         at = stop
-    lax.fori_loop(at, NZ + 3, weights_step, 0)
-    pieces(NZ - 1, NZ)
+    stage_a(NZ)
+    stage_b(NZ - 1)
+    stage_c(NZ - 2)
+    pieces(0, 3)
+    stage_d(NZ - 3)
+    stage_a(NZ + 1)
+    stage_b(NZ)
+    stage_c(NZ - 1)
+    pieces(3, 6)
+    stage_d(NZ - 2)
+    stage_b(NZ + 1)
+    stage_c(NZ)
+    pieces(6, 7)
+    stage_d(NZ - 1)
+    pieces(7, NZ)
+    stage_c(NZ + 1)
 
     hidden = hid[...].astype(BF16).astype(F32)
     hid[...] = hidden
@@ -349,15 +385,18 @@
 
     chunks = NZ // 2
     step, result = ring_sum(part1, s1, r1, rs1s, rs1r, chunks, 1)
-    for c in range(chunks):
-        at = c % 2 * 4 * L
-        share = dot(scaled, kvl[c // 2, :, at : at + 4 * L])
-        for b in range(2):
-            part1[:, 2 * c + b] = share[:, 2 * b * L : 2 * (b + 1) * L].reshape(NZ, slot, 2 * L)
-        step(1, c)
-    for k in range(2, NZ // 2 + 1):
+    for k in range(2):
+        stage_d(NZ + k)
+        mine = (2 * k, 2 * k + 1)
+        for c in mine:
+            at = c % 2 * 4 * L
+            share = dot(scaled, kvl[k, :, at : at + 4 * L])
+            for b in range(2):
+                part1[:, 2 * c + b] = share[:, 2 * b * L : 2 * (b + 1) * L].reshape(NZ, slot, 2 * L)
+            step(1, c)
+    for i in range(2, NZ // 2 + 1):
         for c in range(chunks):
-            step(k, c)
+            step(i, c)
     for r in range(1, NZ):
         j = zmod(d - r)
         remote(ssq_s.at[j], ssq_r.at[j], sqs.at[r], sqr.at[r], dp=j).wait_recv()
@@ -374,10 +413,7 @@
         j = lax.rem(t + r, NT)
         start(remote(kvt.at[:, :, cols(j)], kvh.at[t], ats.at[r], atr.at[r], tensor=j))
     kvh[t] = kvt[:, :, cols(t)]
-    heads = q_ref.shape[1] // L
-    query = jnp.concatenate([q_ref[:, h * L : (h + 1) * L] for h in range(heads)], axis=0)
-    masked = (cot_ref[...].astype(F32) * mask_ref[...].astype(F32)).astype(BF16)
-    grad_out = jnp.concatenate([masked[:, h * L : (h + 1) * L] for h in range(heads)], axis=0)
+    query, grad_out = heads_in[0], heads_in[1]
     for r in range(1, NT):
         j = lax.rem(t + NT - r, NT)
         remote(kvh.at[j], kvh.at[j], ats.at[r], atr.at[r], tensor=j).wait_recv()
@@ -426,7 +462,7 @@
     for c in range(chunks):
         for b in range(2):
             s = 2 * c + b
-            part4[:, s] = dot_nt(grad_hidden, wg[s, :rows, :]).reshape(NZ, slot, rows)
+            part4[:, s] = dot_nt(grad_hidden, wg[s]).reshape(NZ, slot, rows)
         step(1, c)
     for k in range(2, NZ // 2 + 1):
         for c in range(chunks):
@@ -447,7 +483,8 @@
             - normalized * jnp.mean(gain_grad * normalized, -1, keepdims=True)
         )
     ).astype(BF16)
-    gbuf[g] = dot_nt(embed_grad, patch_w[...]).astype(BF16)
+    embed_grad = dot(swap, embed_grad).astype(BF16)
+    gbuf[g] = dot_nt(patch_w[...], embed_grad).astype(BF16)
     for r in range(1, ng):
         start(remote(gbuf.at[g], gbuf.at[g], grs.at[r], grr.at[r], group=lax.rem(g + r, ng)))
     for r in range(1, ng):
@@ -463,23 +500,33 @@
         j = lax.rem(t + NT - r, NT)
         remote(sqb.at[j], sqb.at[j], fs.at[r], fr.at[r], tensor=j).wait_recv()
     squares = jnp.sum(sqb[...], axis=0)[:1, :1]
-    out_ref[...] = jnp.tanh(gradient * lax.rsqrt(squares / n_pixels + 1e-06))
+    direction = jnp.tanh(gradient * lax.rsqrt(squares / n_pixels + 1e-06))
+    dir_ref[...] = direction
+    stores = [pltpu.make_async_copy(dir_ref, dir_hbm.at[:, 0, :], local_sem.at[5])]
+    stores[0].start()
+    adv_ref[...] = jnp.clip(pix[...] + step_ref[...] * direction, 0.0, 1.0)
+    stores.append(pltpu.make_async_copy(adv_ref, adv_hbm.at[:, 0, :], local_sem.at[6]))
+    stores[1].start()
+    for c in stores:
+        c.wait()
 
     for copy in sent:
         copy.wait_send()
 
     def drain(p, carry):
-        for kind in range(len(kinds)):
+        for kind in range(10):
             xy(kind, p).wait_send()
 
         @pl.when(p > 0)
         def _():
-            for which in range(3):
-                z_out(p, which).wait_send()
+            z_copy(p, 0).wait_send()
 
         return carry
 
     lax.fori_loop(0, NZ, drain, 0)
+    for p in (NZ, NZ + 1):
+        for kind in range(10):
+            xy(kind, p).wait_send()
 
 
 def body(
@@ -501,17 +548,17 @@
     rows, width = merger_weight.shape[1:]
     vwidth = patch_weight.shape[2]
     half = NZ // 2
-    turned = images[0].reshape(slot, 4, pixels).transpose(1, 0, 2).reshape(patches, pixels)
     dma = pltpu.SemaphoreType.DMA
     vmem = pl.BlockSpec(memory_space=pltpu.VMEM)
     anywhere = pl.BlockSpec(memory_space=pl.ANY)
-    direction = pl.pallas_call(
+    flipped = jax.ShapeDtypeStruct((pixels, 1, patches), F32)
+    adversarial, direction = pl.pallas_call(
         functools.partial(kernel, ng, float(NT * patches * pixels)),
-        out_shape=jax.ShapeDtypeStruct((patches, pixels), F32),
-        in_specs=[vmem, anywhere, vmem, anywhere, vmem, anywhere, vmem, vmem, vmem],
-        out_specs=vmem,
+        out_shape=(flipped, flipped),
+        in_specs=[anywhere, anywhere, vmem, anywhere, vmem, anywhere, vmem, vmem, vmem, vmem],
+        out_specs=(anywhere, anywhere),
         scratch_shapes=[
-            pltpu.VMEM((NZ, rows + 2 * L, NT * L), BF16),
+            pltpu.VMEM((NZ, rows, NT * L), BF16),
             pltpu.VMEM((2, NZ * L, NT * L), BF16),
             pltpu.VMEM((NZ, NZ, slot, rows), BF16),
             pltpu.VMEM((NZ * slot, NT * L), F32),
@@ -530,14 +577,18 @@
             pltpu.VMEM((2, half, NZ, slot, rows), BF16),
             pltpu.VMEM((2, half, NZ, slot, rows), BF16),
             pltpu.VMEM((patches, vwidth), F32),
-            pltpu.VMEM((ng, patches, pixels), BF16),
+            pltpu.VMEM((ng, pixels, patches), BF16),
             pltpu.VMEM((NT, 8, L), F32),
             pltpu.VMEM((pixels, vwidth), BF16),
-            dma((4,)),
+            pltpu.VMEM((2, NZ * slot, L), BF16),
+            pltpu.VMEM((pixels, patches), F32),
+            pltpu.VMEM((pixels, patches), F32),
+            pltpu.VMEM((pixels, patches), F32),
+            dma((7,)),
             dma((3, NZ)),
             dma((3, NZ)),
-            dma((10, NZ)),
-            dma((10, NZ)),
+            dma((10, NZ + 2)),
+            dma((10, NZ + 2)),
             dma((2, half, 2)),
             dma((2, half, 2)),
             dma((2, half, half)),
@@ -563,7 +614,7 @@
             collective_id=0, has_side_effects=True, vmem_limit_bytes=60 * 1024 * 1024
         ),
     )(
-        turned.astype(BF16),
+        images.transpose(2, 0, 1),
         patch_weight[0],
         vision_norm_gain,
         merger_weight[0],
@@ -572,10 +623,9 @@
         queries[0, 0],
         cotangent[0, 0],
         member_mask,
+        step_size[None],
     )
-    direction = direction.reshape(4, slot, pixels).transpose(1, 0, 2).reshape(images.shape)
-    adversarial = jnp.clip(images + step_size[:, None, None] * direction, 0.0, 1.0)
-    return adversarial, direction
+    return adversarial.transpose(1, 2, 0), direction.transpose(1, 2, 0)
 
 
 def solution(mesh):

time: 201 us -> 195 us (0.970)
  Pallas kernels: 193 us -> 189 us
    pallas_call x1, Pallas kernels: 193 us -> 189 us  [body(): pl.pallas_call(functools.partial(kernel, ng, float(NT * patches * pixels)...]
where the time goes in v4:
time: 195 us; the launch traced here: 194 us
  Pallas kernels  189 us (97%)
  local copies, waits for them, and re-layouts  3.4 us (2%)
    pallas_call x1, Pallas kernels, body(): pl.pallas_call(functools.partial(kernel, ng, float(NT * patches * pixels)...  189 us

profile of v4, /device:TPU:1, one launch (start us, length us, event | category | flops | bytes accessed | tf_op | source)
XLA Modules:
  0.0 194.3 jit_solution(17223159792564955384)
XLA Ops:
  1.9 189.0 %shard_map.113 = (f32[588,1,128]{2,1,0:T(1,128)}, f32[588,1,128]{2,1,0:T(1,128)}) custom-call(f32[588,1,128]{2,1,0:T(1,128)} %bitcast.13, bf16[588,1280]{1,0:T(8,128)(2,1)} %bitcast.10, f32[1,1280]{1,0:T(1,128)} %vgain.1, bf16[640,1024]{1,0:T(8,128)(2,1)} %bitcast.11, f32[1,8192]{1,0:T(1,128)} %gain_ref.1, bf16[2,1024,128]{2,1,0:T(8,128)(2,1)} %bitcast.12, ...), custom_call_target="tpu_custom_call" | custom-call | tf_op jit(solution)/shard_map/pallas_call | solution.py:555
  190.9 1.7 copy.16
  192.6 1.7 copy.17

commit v5 on v4

--- a/solution.py
+++ b/solution.py
@@ -39,8 +39,6 @@
     q_ref,
     cot_ref,
     mask_ref,
-    step_ref,
-    adv_hbm,
     dir_hbm,
     wg,
     kvl,
@@ -66,7 +64,6 @@
     patch_w,
     heads_in,
     pix,
-    adv_ref,
     dir_ref,
     local_sem,
     zs,
@@ -224,7 +221,6 @@
     natural = lax.broadcasted_iota(jnp.int32, (patches, patches), 0)
     turned = lax.broadcasted_iota(jnp.int32, (patches, patches), 1)
     per = patches // slot
-    swap = jnp.where(turned == lax.rem(natural, per) * slot + natural // per, 1.0, 0.0).astype(BF16)
     back = jnp.where(natural == lax.rem(turned, per) * slot + turned // per, 1.0, 0.0).astype(BF16)
     load_pixels.wait()
     pixels = dot_nt(back, pix[...].astype(BF16)).astype(BF16)
@@ -467,32 +463,34 @@
     for k in range(2, NZ // 2 + 1):
         for c in range(chunks):
             step(k, c)
-    blocks = []
     for c in range(chunks):
         value = result(c)
-        blocks.append(jnp.concatenate([value[0], value[1]], axis=-1))
-    grad_visual = jnp.concatenate(blocks, axis=0)
-
-    gain_grad = grad_visual * vgain[...]
-    normalized = xhat[...]
-    embed_grad = (
-        inv_dev
-        * (
-            gain_grad
-            - jnp.mean(gain_grad, -1, keepdims=True)
-            - normalized * jnp.mean(gain_grad * normalized, -1, keepdims=True)
-        )
-    ).astype(BF16)
-    embed_grad = dot(swap, embed_grad).astype(BF16)
-    gbuf[g] = dot_nt(patch_w[...], embed_grad).astype(BF16)
-    for r in range(1, ng):
-        start(remote(gbuf.at[g], gbuf.at[g], grs.at[r], grr.at[r], group=lax.rem(g + r, ng)))
-    for r in range(1, ng):
-        j = lax.rem(g + ng - r, ng)
-        remote(gbuf.at[j], gbuf.at[j], grs.at[r], grr.at[r], group=j).wait_recv()
-    gradient = gbuf[0].astype(F32)
-    for m in range(1, ng):
-        gradient = gradient + gbuf[m].astype(F32)
+        gain_grad = jnp.concatenate([value[0], value[1]], axis=-1) * vgain[...]
+        mine = pl.ds(c * slot, slot)
+        normalized = xhat[mine, :]
+        embed_grad = (
+            inv_dev[c * slot : (c + 1) * slot]
+            * (
+                gain_grad
+                - jnp.mean(gain_grad, -1, keepdims=True)
+                - normalized * jnp.mean(gain_grad * normalized, -1, keepdims=True)
+            )
+        ).astype(BF16)
+        gbuf[g, mine] = dot_nt(embed_grad, patch_w[...]).astype(BF16)
+        for r in range(1, ng):
+            view = gbuf.at[g, mine]
+            start(remote(view, view, grs.at[r, c], grr.at[r, c], group=lax.rem(g + r, ng)))
+    for c in range(chunks):
+        for r in range(1, ng):
+            j = lax.rem(g + ng - r, ng)
+            view = gbuf.at[j, pl.ds(c * slot, slot)]
+            remote(view, view, grs.at[r, c], grr.at[r, c], group=j).wait_recv()
+    gradient = lax.dot_general(
+        gbuf[...].reshape(ng * patches, -1),
+        jnp.concatenate([back] * ng, axis=0),
+        (((0,), (0,)), ((), ())),
+        preferred_element_type=F32,
+    )
     sqb[t] = jnp.broadcast_to(jnp.sum(gradient * gradient), (8, L))
     for r in range(1, NT):
         start(remote(sqb.at[t], sqb.at[t], fs.at[r], fr.at[r], tensor=lax.rem(t + r, NT)))
@@ -500,15 +498,10 @@
         j = lax.rem(t + NT - r, NT)
         remote(sqb.at[j], sqb.at[j], fs.at[r], fr.at[r], tensor=j).wait_recv()
     squares = jnp.sum(sqb[...], axis=0)[:1, :1]
-    direction = jnp.tanh(gradient * lax.rsqrt(squares / n_pixels + 1e-06))
-    dir_ref[...] = direction
-    stores = [pltpu.make_async_copy(dir_ref, dir_hbm.at[:, 0, :], local_sem.at[5])]
-    stores[0].start()
-    adv_ref[...] = jnp.clip(pix[...] + step_ref[...] * direction, 0.0, 1.0)
-    stores.append(pltpu.make_async_copy(adv_ref, adv_hbm.at[:, 0, :], local_sem.at[6]))
-    stores[1].start()
-    for c in stores:
-        c.wait()
+    dir_ref[...] = gradient * lax.rsqrt(squares / n_pixels + 1e-06)
+    store = pltpu.make_async_copy(dir_ref, dir_hbm.at[:, 0, :], local_sem.at[5])
+    store.start()
+    store.wait()
 
     for copy in sent:
         copy.wait_send()
@@ -551,12 +544,11 @@
     dma = pltpu.SemaphoreType.DMA
     vmem = pl.BlockSpec(memory_space=pltpu.VMEM)
     anywhere = pl.BlockSpec(memory_space=pl.ANY)
-    flipped = jax.ShapeDtypeStruct((pixels, 1, patches), F32)
-    adversarial, direction = pl.pallas_call(
+    normed = pl.pallas_call(
         functools.partial(kernel, ng, float(NT * patches * pixels)),
-        out_shape=(flipped, flipped),
-        in_specs=[anywhere, anywhere, vmem, anywhere, vmem, anywhere, vmem, vmem, vmem, vmem],
-        out_specs=(anywhere, anywhere),
+        out_shape=jax.ShapeDtypeStruct((pixels, 1, patches), F32),
+        in_specs=[anywhere, anywhere, vmem, anywhere, vmem, anywhere, vmem, vmem, vmem],
+        out_specs=anywhere,
         scratch_shapes=[
             pltpu.VMEM((NZ, rows, NT * L), BF16),
             pltpu.VMEM((2, NZ * L, NT * L), BF16),
@@ -577,14 +569,13 @@
             pltpu.VMEM((2, half, NZ, slot, rows), BF16),
             pltpu.VMEM((2, half, NZ, slot, rows), BF16),
             pltpu.VMEM((patches, vwidth), F32),
-            pltpu.VMEM((ng, pixels, patches), BF16),
+            pltpu.VMEM((ng, patches, pixels), BF16),
             pltpu.VMEM((NT, 8, L), F32),
             pltpu.VMEM((pixels, vwidth), BF16),
             pltpu.VMEM((2, NZ * slot, L), BF16),
             pltpu.VMEM((pixels, patches), F32),
             pltpu.VMEM((pixels, patches), F32),
-            pltpu.VMEM((pixels, patches), F32),
-            dma((7,)),
+            dma((6,)),
             dma((3, NZ)),
             dma((3, NZ)),
             dma((10, NZ + 2)),
@@ -605,8 +596,8 @@
             dma((NZ,)),
             dma((2, half, half)),
             dma((2, half, half)),
-            dma((max(ng, 2),)),
-            dma((max(ng, 2),)),
+            dma((max(ng, 2), half)),
+            dma((max(ng, 2), half)),
             dma((NT,)),
             dma((NT,)),
         ],
@@ -623,9 +614,10 @@
         queries[0, 0],
         cotangent[0, 0],
         member_mask,
-        step_size[None],
     )
-    return adversarial.transpose(1, 2, 0), direction.transpose(1, 2, 0)
+    direction = jnp.tanh(normed.transpose(1, 2, 0))
+    adversarial = jnp.clip(images + step_size[:, None, None] * direction, 0.0, 1.0)
+    return adversarial, direction
 
 
 def solution(mesh):

time: 195 us -> 191 us (0.979)
  local copies, waits for them, and re-layouts: 3.4 us -> 0.01 us
  other arithmetic: 0 us -> 2.25 us
  Pallas kernels: 189 us -> 187 us
    unnamed x2, local copies, waits for them, and re-layouts: 3.4 us -> 0.01 us
    min x0 -> x1, other arithmetic: none -> 2.25 us  [body(): jnp.clip(images + step_size[:, None, None] * direction, 0.0, 1.0)]
    pallas_call x1, Pallas kernels: 189 us -> 187 us  [body(): pl.pallas_call(functools.partial(kernel, ng, float(NT * patches * pixels)...]
where the time goes in v5:
time: 191 us
  Pallas kernels  187 us (98%)
  other arithmetic  2.25 us (1%)
  between operations  1.95 us (1%)
    pallas_call x1, Pallas kernels, body(): pl.pallas_call(functools.partial(kernel, ng, float(NT * patches * pixels)...  187 us

profile of v5, /device:TPU:1, one launch (start us, length us, event | category | flops | bytes accessed | tf_op | source)
XLA Modules:
  0.0 191.1 jit_solution(16802715697591536849)
XLA Ops:
  1.9 0.0 copy-start
  1.9 186.9 %shard_map.113 = f32[588,1,128]{2,1,0:T(1,128)} custom-call(f32[588,1,128]{2,1,0:T(1,128)} %bitcast.13, bf16[588,1280]{1,0:T(8,128)(2,1)} %bitcast.11, f32[1,1280]{1,0:T(1,128)} %vgain.1, bf16[640,1024]{1,0:T(8,128)(2,1)} %bitcast.12, f32[1,8192]{1,0:T(1,128)} %gain_ref.1, bf16[2,1024,128]{2,1,0:T(8,128)(2,1)} %bitcast.14, bf16[32,1024]{1,0:T(8,128)(2,1)} %bitcast.15, ...), custom_call_target="tpu_custom_call" | custom-call | tf_op jit(solution)/shard_map/pallas_call | solution.py:547
  188.8 0.0 copy-done
  188.9 2.2 %add_clamp_fusion = (f32[1,128,588]{1,0,2:T(1,128)}, f32[1,128,588]{1,0,2:T(1,128)}) fusion(f32[1,128,588]{1,0,2:T(1,128)S(1)} %copy-done, f32[]{:T(128)} %bitcast.10, f32[588,1,128]{2,1,0:T(1,128)} %shard_map.113), kind=kLoop, calls=%fused_computation | loop fusion | flops 225792 | bytes 1204228 | tf_op jit(solution)/shard_map/jit(clip)/min | solution.py:619
Async XLA Ops:
  1.9 186.9 %copy-start = (f32[1,128,588]{1,0,2:T(1,128)S(1)}, f32[1,128,588]{1,0,2:T(1,128)}, u32[]{:S(2)}) copy-start(f32[1,128,588]{1,0,2:T(1,128)} %param.10) | copy-start | bytes 903172

commit v6 on v5

--- a/solution.py
+++ b/solution.py
@@ -143,7 +143,7 @@
     xo = (1 - x) * NY
     across = xo + y
     def kinds(height):
-        part = height // 6 // 16 * 16
+        part = height * 9 // 50 // 16 * 16
         whole, lo, hi = (0, height), (0, height // 2), (height // 2, height // 2)
         first, rest = (0, part), (part, height - part)
         return (

time: 191 us -> 193 us (1.010)
  Pallas kernels: 187 us -> 189 us
where the time goes in v6:
time: 193 us
  Pallas kernels  189 us (98%)
  other arithmetic  2.25 us (1%)
  between operations  1.95 us (1%)
    pallas_call x1, Pallas kernels, body(): pl.pallas_call(functools.partial(kernel, ng, float(NT * patches * pixels)...  189 us

profile of v6, /device:TPU:1, one launch (start us, length us, event | category | flops | bytes accessed | tf_op | source)
XLA Modules:
  0.0 193.0 jit_solution(4082065333786405031)
XLA Ops:
  1.9 0.0 copy-start
  1.9 188.8 %shard_map.113 = f32[588,1,128]{2,1,0:T(1,128)} custom-call(f32[588,1,128]{2,1,0:T(1,128)} %bitcast.13, bf16[588,1280]{1,0:T(8,128)(2,1)} %bitcast.11, f32[1,1280]{1,0:T(1,128)} %vgain.1, bf16[640,1024]{1,0:T(8,128)(2,1)} %bitcast.12, f32[1,8192]{1,0:T(1,128)} %gain_ref.1, bf16[2,1024,128]{2,1,0:T(8,128)(2,1)} %bitcast.14, bf16[32,1024]{1,0:T(8,128)(2,1)} %bitcast.15, ...), custom_call_target="tpu_custom_call" | custom-call | tf_op jit(solution)/shard_map/pallas_call | solution.py:547
  190.8 0.0 copy-done
  190.8 2.2 %add_clamp_fusion = (f32[1,128,588]{1,0,2:T(1,128)}, f32[1,128,588]{1,0,2:T(1,128)}) fusion(f32[1,128,588]{1,0,2:T(1,128)S(1)} %copy-done, f32[]{:T(128)} %bitcast.10, f32[588,1,128]{2,1,0:T(1,128)} %shard_map.113), kind=kLoop, calls=%fused_computation | loop fusion | flops 225792 | bytes 1204228 | tf_op jit(solution)/shard_map/jit(clip)/min | solution.py:619
Async XLA Ops:
  1.9 188.8 %copy-start = (f32[1,128,588]{1,0,2:T(1,128)S(1)}, f32[1,128,588]{1,0,2:T(1,128)}, u32[]{:S(2)}) copy-start(f32[1,128,588]{1,0,2:T(1,128)} %param.10) | copy-start | bytes 903172
